TPU v7x, 32 devices: a whole 2x2x4 slice. The times are simulated.
32 devices in a mesh: parts: 2 (over y), tile: 4 (over z), ch: 2 (over x), sub: 2 (over core).
Axes of the slice: x: 2, y: 2, z: 4, core: 2. Of those that a mesh axis runs over, the one named last changes fastest.
Arguments:
- feats: bfloat16 [8, 4, 64, 256], P(('parts', 'tile'), ('ch', 'sub')), parts along dimension 0, may hold values from -6 to 6
- weight1: bfloat16 [27, 64, 64], replicated, may hold values from -0.15625 to 0.15625
- bias1: float32 [64], replicated, may hold values from -3 to 3
- weight2: bfloat16 [27, 64, 64], replicated, may hold values from -0.15625 to 0.15625
- bias2: float32 [64], replicated, may hold values from -3 to 3
- cotangent: bfloat16 [8, 4, 64, 256], P(('parts', 'tile'), ('ch', 'sub')), parts along dimension 0, may hold values from -6 to 6
- neighbors: int32 [8, 4, 27, 256], P(('parts', 'tile'), ('ch', 'sub')), parts along dimension 0, may hold values from 0 to 2304, as said below
- shell: int32 [8, 4, 2, 2, 128], P(('parts', 'tile'), ('ch', 'sub')), parts along dimension 0, may hold values from 0 to 256, as said below
Outputs:
- grad_feats: float32 [8, 4, 64, 256], P(('parts', 'tile'), ('ch', 'sub')), parts along dimension 0
- grad_w1: float32 [54, 64, 64], P('parts'), parts along dimension 0
- grad_b1: float32 [128], P('parts'), parts along dimension 0
- grad_w2: float32 [54, 64, 64], P('parts'), parts along dimension 0
- grad_b2: float32 [128], P('parts'), parts along dimension 0
There are 2 independent parts, one for each index of `parts`. A program takes and returns all parts, laid end to end along the dimension named above; an argument that names none is the same for every part. Nothing has to cross between parts.
Inputs may be any that keep to these rules, and one draw needn't show every extreme that they name: Voxels stand in columns of a grid of 32 x 4 * 8 columns, 4 at distinct heights in each; tile (tx, ty) holds the columns of its 8 x 8 square. neighbors[tx, ty, k, v] is the frame row (step frame) of the voxel at v's position plus offset (dx, dy, dz), k = 9 (dx + 1) + 3 (dy + 1) + (dz + 1), or 2304 if that position holds no voxel; if v's offset k points at u, u's offset 26 - k points at v. shell[tx, ty, a, b] lists, in its first (7) * 4 slots, the rows of the tile's voxels in the outermost columns of quadrant (a, b) of its square, 4 for each of 7 columns, each such voxel once; the other slots hold 256.
All inputs are finite; a program needn't handle non-finite values.
Results may differ from a plain program's by a relative error of at most 0.005.
Values may be sent and summed in bfloat16 or wider, within the bound.
A program may use at most 64 MiB of HBM per device.

v0:
```python
import math

import jax
import jax.numpy as jnp
from jax import lax
from jax.sharding import PartitionSpec as P


def padded(value, sides, width):
    for axis, dim in sides:
        peers, length = (lax.axis_size(axis), value.shape[dim])
        up = [(i, (i + 1) % peers) for i in range(peers - 1)]
        down = [(j, i) for i, j in up]
        last = lax.slice_in_dim(value, length - width, length, axis=dim)
        initial = lax.slice_in_dim(value, 0, width, axis=dim)
        before = lax.ppermute(last, axis, up)
        after = lax.ppermute(initial, axis, down)
        value = jnp.concatenate([before, value, after], axis=dim)
    return value


def silu_slope(values):
    sigmoid = jax.nn.sigmoid(values)
    return sigmoid * (1.0 + values * (1.0 - sigmoid))


def build_frame(source, shell_rows):
    buckets = jnp.take(source, shell_rows, axis=1, mode="fill", fill_value=0)
    cycle_rows = padded(buckets, (("tile", 1), (("ch", "sub"), 2)), 1)
    return jnp.concatenate([source, cycle_rows.reshape(source.shape[0], -1)], axis=1)


def gradient_frame(source, shell_rows):
    buckets = jnp.take(source, shell_rows, axis=1, mode="fill", fill_value=0)
    cycle_rows = padded(buckets, (("tile", 1), (("ch", "sub"), 2)), 1)
    return jnp.concatenate([source, cycle_rows.reshape(source.shape[0], -1)], axis=1)


def gather_offsets(framed, near_rows):
    return [
        jnp.take(framed, near_rows[9 * k : 9 * k + 9], axis=1, mode="fill", fill_value=0)
        for k in range(3)
    ]


def convolve_picked(picked_blocks, weight):
    running = jnp.zeros((weight.shape[2], picked_blocks[0].shape[2]), jnp.float32)
    for k in range(3):
        running = running + jnp.einsum(
            "kio,ikr->or",
            weight[9 * k : 9 * k + 9],
            picked_blocks[k],
            preferred_element_type=jnp.float32,
        )
    return running


def weight_grad(picked_blocks, gradient):
    pieces = []
    for k in range(3):
        pieces.append(
            jnp.einsum(
                "ikr,or->kio", picked_blocks[k], gradient, preferred_element_type=jnp.float32
            )
        )
    return jnp.concatenate(pieces, axis=0)


def per_device(feats, weight1, bias1, weight2, bias2, cotangent, neighbors, shell):
    inputs = feats[0, 0]
    upstream = cotangent[0, 0]
    near_rows = neighbors[0, 0]
    shell_rows = shell[0, 0]
    flipped = near_rows[::-1]
    voxel_total = inputs.shape[1] * lax.axis_size("tile") * lax.axis_size(("ch", "sub"))
    grad_scale = 1.0 / math.sqrt(voxel_total)
    picked_in = gather_offsets(build_frame(inputs, shell_rows), near_rows)
    first = convolve_picked(picked_in, weight1) + bias1[:, None]
    hidden = jax.nn.silu(first).astype(jnp.bfloat16)
    picked_hidden = gather_offsets(build_frame(hidden, shell_rows), near_rows)
    second = convolve_picked(picked_hidden, weight2) + bias2[:, None]
    summed = inputs.astype(jnp.float32) + second
    grad_out = (upstream.astype(jnp.float32) * silu_slope(summed)).astype(jnp.bfloat16)
    grad_w2 = weight_grad(picked_hidden, grad_out)
    grad_b2 = jnp.sum(grad_out.astype(jnp.float32), axis=1)
    picked_grad = gather_offsets(gradient_frame(grad_out, shell_rows), flipped)
    back_second = convolve_picked(picked_grad, jnp.swapaxes(weight2, 1, 2))
    grad_pre = (back_second * silu_slope(first)).astype(jnp.bfloat16)
    picked_pre = gather_offsets(gradient_frame(grad_pre, shell_rows), flipped)
    back_first = convolve_picked(picked_pre, jnp.swapaxes(weight1, 1, 2))
    grad_feats = grad_out.astype(jnp.float32) + back_first
    grad_w1 = weight_grad(picked_in, grad_pre)
    grad_b1 = jnp.sum(grad_pre.astype(jnp.float32), axis=1)
    grad_w1, grad_b1, grad_w2, grad_b2 = lax.psum(
        (grad_w1, grad_b1, grad_w2, grad_b2), ("tile", "ch", "sub")
    )
    return (
        grad_feats[None, None],
        grad_w1 * grad_scale,
        grad_b1 * grad_scale,
        grad_w2 * grad_scale,
        grad_b2 * grad_scale,
    )


def solution(mesh):
    placed = (
        P(("parts", "tile"), ("ch", "sub"), None, None),
        P(),
        P(),
        P(),
        P(),
        P(("parts", "tile"), ("ch", "sub"), None, None),
        P(("parts", "tile"), ("ch", "sub"), None, None),
        P(("parts", "tile"), ("ch", "sub"), None, None, None),
    )
    return jax.shard_map(
        per_device,
        mesh=mesh,
        in_specs=placed,
        out_specs=(
            P(("parts", "tile"), ("ch", "sub"), None, None),
            P("parts", None, None),
            P("parts"),
            P("parts", None, None),
            P("parts"),
        ),
        check_vma=False,
    )
```

profile of v0, /device:TPU:0, one launch (start us, length us, event | category | flops | bytes accessed | tf_op | source)
XLA Modules:
  0.0 264.1 jit_solution(7395013165243741355)
XLA Ops:
  7.2 0.7 compare_select_fusion.6
  8.0 0.7 compare_and_fusion.6
  8.7 0.9 copy.14
  9.5 1.3 gather_fusion
  11.0 1.3 collective-permute-start.1
  12.3 5.6 %collective-permute-start = (bf16[64,1,2,128]{0,3,2,1:T(8,128)(2,1)S(1)}, bf16[64,1,2,128]{0,3,2,1:T(8,128)(2,1)S(1)}, u32[]{:S(2)}, u32[]{:S(2)}) collective-permute-start(bf16[64,1,2,128]{0,3,2,1:T(8,128)(2,1)S(1)} %get-tuple-element.30), channel_id=1, source_target_pairs={{0,4},{4,8},{8,12},{1,5},{5,9},{9,13},{2,6},{6,10},{10,14},{3,7},{... | collective-permute-start | bytes 98312 | tf_op jit(solution)/shard_map/ppermute | solution.py:16
  18.5 1.3 collective-permute-done
  19.9 1.3 collective-permute-start.3
  21.2 3.0 %collective-permute-start.2 = (bf16[64,4,1,128]{0,3,2,1:T(8,128)(2,1)S(1)}, bf16[64,4,1,128]{0,3,2,1:T(8,128)(2,1)S(1)}, u32[]{:S(2)}, u32[]{:S(2)}) collective-permute-start(bf16[64,4,1,128]{0,3,2,1:T(8,128)(2,1)S(1)} %get-tuple-element.22), channel_id=1, source_target_pairs={{0,1},{1,2},{2,3},{4,5},{5,6},{6,7},{8,9},{9,10},{10,11},{12,13},{... | collective-permute-start | bytes 196616 | tf_op jit(solution)/shard_map/ppermute | solution.py:16
  24.3 0.9 collective-permute-done.2
  25.5 4.7 %gather_fusion.1 = bf16[2304,64]{1,0:T(8,128)(2,1)S(1)} fusion(bf16[64,2304]{0,1:T(8,128)(2,1)S(1)} %pad_maximum_fusion.2, s32[3072]{0:T(1024)S(1)} %pad_clamp_fusion.5), kind=kCustom, calls=%fused_computation.1.clone | custom fusion | bytes 599040 | tf_op jit(solution)/shard_map/jit(_take)/gather | solution.py:41
  30.1 0.2 copy.15
  30.4 4.7 %gather_fusion.2 = bf16[2304,64]{1,0:T(8,128)(2,1)S(1)} fusion(bf16[64,2304]{0,1:T(8,128)(2,1)S(1)} %pad_maximum_fusion.2, s32[3072]{0:T(1024)S(1)} %pad_clamp_fusion.4), kind=kCustom, calls=%fused_computation.5.clone | custom fusion | bytes 599040 | tf_op jit(solution)/shard_map/jit(_take)/gather | solution.py:41
  35.3 4.7 %gather_fusion.3 = bf16[2304,64]{1,0:T(8,128)(2,1)S(1)} fusion(bf16[64,2304]{0,1:T(8,128)(2,1)S(1)} %pad_maximum_fusion.2, s32[3072]{0:T(1024)S(1)} %pad_clamp_fusion.3), kind=kCustom, calls=%fused_computation.6.clone | custom fusion | bytes 599040 | tf_op jit(solution)/shard_map/jit(_take)/gather | solution.py:41
  40.9 0.8 multiply_convert_fusion
  41.9 1.3 gather_fusion.4
  43.4 1.3 collective-permute-start.5
  44.7 4.9 %collective-permute-start.4 = (bf16[64,1,2,128]{0,3,2,1:T(8,128)(2,1)S(1)}, bf16[64,1,2,128]{0,3,2,1:T(8,128)(2,1)S(1)}, u32[]{:S(2)}, u32[]{:S(2)}) collective-permute-start(bf16[64,1,2,128]{0,3,2,1:T(8,128)(2,1)S(1)} %get-tuple-element.28), channel_id=1, source_target_pairs={{0,4},{4,8},{8,12},{1,5},{5,9},{9,13},{2,6},{6,10},{10,14},{3,7},{... | collective-permute-start | bytes 98312 | tf_op jit(solution)/shard_map/ppermute | solution.py:16
  49.6 0.3 collective-permute-done.5
  49.9 1.6 collective-permute-done.4
  51.6 1.3 collective-permute-start.7
  52.9 4.2 %collective-permute-start.6 = (bf16[64,4,1,128]{0,3,2,1:T(8,128)(2,1)S(1)}, bf16[64,4,1,128]{0,3,2,1:T(8,128)(2,1)S(1)}, u32[]{:S(2)}, u32[]{:S(2)}) collective-permute-start(bf16[64,4,1,128]{0,3,2,1:T(8,128)(2,1)S(1)} %get-tuple-element.20), channel_id=1, source_target_pairs={{0,1},{1,2},{2,3},{4,5},{5,6},{6,7},{8,9},{9,10},{10,11},{12,13},{... | collective-permute-start | bytes 196616 | tf_op jit(solution)/shard_map/ppermute | solution.py:16
  57.1 0.9 collective-permute-done.6
  58.3 4.7 %gather_fusion.5 = bf16[2304,64]{1,0:T(8,128)(2,1)S(1)} fusion(bf16[64,2304]{0,1:T(8,128)(2,1)S(1)} %pad_maximum_fusion.3, s32[3072]{0:T(1024)S(1)} %pad_clamp_fusion.5), kind=kCustom, calls=%fused_computation.7.clone | custom fusion | bytes 599040 | tf_op jit(solution)/shard_map/jit(_take)/gather | solution.py:41
  63.0 4.7 %gather_fusion.6 = bf16[2304,64]{1,0:T(8,128)(2,1)S(1)} fusion(bf16[64,2304]{0,1:T(8,128)(2,1)S(1)} %pad_maximum_fusion.3, s32[3072]{0:T(1024)S(1)} %pad_clamp_fusion.4), kind=kCustom, calls=%fused_computation.8.clone | custom fusion | bytes 599040 | tf_op jit(solution)/shard_map/jit(_take)/gather | solution.py:41
  67.6 4.7 %gather_fusion.7 = bf16[2304,64]{1,0:T(8,128)(2,1)S(1)} fusion(bf16[64,2304]{0,1:T(8,128)(2,1)S(1)} %pad_maximum_fusion.3, s32[3072]{0:T(1024)S(1)} %pad_clamp_fusion.3), kind=kCustom, calls=%fused_computation.9.clone | custom fusion | bytes 599040 | tf_op jit(solution)/shard_map/jit(_take)/gather | solution.py:41
  73.0 0.8 copy-done.4
  74.3 0.3 copy-done.5
  74.6 0.3 convert_reduce_fusion
  75.0 0.3 convolution_bitcast_fusion
  75.3 0.3 convolution_bitcast_fusion.1
  75.6 1.3 gather_fusion.8
  77.1 1.3 collective-permute-start.9
  78.4 4.6 %collective-permute-start.8 = (bf16[64,1,2,128]{0,3,2,1:T(8,128)(2,1)S(1)}, bf16[64,1,2,128]{0,3,2,1:T(8,128)(2,1)S(1)}, u32[]{:S(2)}, u32[]{:S(2)}) collective-permute-start(bf16[64,1,2,128]{0,3,2,1:T(8,128)(2,1)S(1)} %get-tuple-element.26), channel_id=1, source_target_pairs={{0,4},{4,8},{8,12},{1,5},{5,9},{9,13},{2,6},{6,10},{10,14},{3,7},{... | collective-permute-start | bytes 98312 | tf_op jit(solution)/shard_map/ppermute | solution.py:16
  83.0 0.3 convolution_bitcast_fusion.2
  83.3 1.6 collective-permute-done.8
  85.0 1.3 collective-permute-start.11
  86.3 6.4 %collective-permute-start.10 = (bf16[64,4,1,128]{0,3,2,1:T(8,128)(2,1)S(1)}, bf16[64,4,1,128]{0,3,2,1:T(8,128)(2,1)S(1)}, u32[]{:S(2)}, u32[]{:S(2)}) collective-permute-start(bf16[64,4,1,128]{0,3,2,1:T(8,128)(2,1)S(1)} %get-tuple-element.18), channel_id=1, source_target_pairs={{0,1},{1,2},{2,3},{4,5},{5,6},{6,7},{8,9},{9,10},{10,11},{12,13},{... | collective-permute-start | bytes 196616 | tf_op jit(solution)/shard_map/ppermute | solution.py:16
  92.7 1.0 pad_maximum_fusion.1
  94.0 4.7 %gather_fusion.11 = bf16[2304,64]{1,0:T(8,128)(2,1)S(1)} fusion(bf16[64,2304]{0,1:T(8,128)(2,1)S(1)} %pad_maximum_fusion.4, s32[3072]{0:T(1024)S(1)} %pad_clamp_fusion), kind=kCustom, calls=%fused_computation.12.clone | custom fusion | bytes 599040 | tf_op jit(solution)/shard_map/jit(_take)/gather | solution.py:41
  98.9 4.7 %gather_fusion.10 = bf16[2304,64]{1,0:T(8,128)(2,1)S(1)} fusion(bf16[64,2304]{0,1:T(8,128)(2,1)S(1)} %pad_maximum_fusion.4, s32[3072]{0:T(1024)S(1)} %pad_clamp_fusion.1), kind=kCustom, calls=%fused_computation.11.clone | custom fusion | bytes 599040 | tf_op jit(solution)/shard_map/jit(_take)/gather | solution.py:41
  103.8 4.7 %gather_fusion.9 = bf16[2304,64]{1,0:T(8,128)(2,1)S(1)} fusion(bf16[64,2304]{0,1:T(8,128)(2,1)S(1)} %pad_maximum_fusion.4, s32[3072]{0:T(1024)S(1)} %pad_clamp_fusion.2), kind=kCustom, calls=%fused_computation.10.clone | custom fusion | bytes 599040 | tf_op jit(solution)/shard_map/jit(_take)/gather | solution.py:41
  109.2 0.4 copy-done.10
  109.6 0.3 convert_reduce_fusion.1
  110.0 0.3 convolution_bitcast_fusion.3
  110.3 0.3 convolution_bitcast_fusion.4
  110.5 0.3 convolution_bitcast_fusion.5
  110.8 1.3 gather_fusion.12
  112.3 1.3 collective-permute-start.13
  113.6 4.6 %collective-permute-start.12 = (bf16[64,1,2,128]{0,3,2,1:T(8,128)(2,1)S(1)}, bf16[64,1,2,128]{0,3,2,1:T(8,128)(2,1)S(1)}, u32[]{:S(2)}, u32[]{:S(2)}) collective-permute-start(bf16[64,1,2,128]{0,3,2,1:T(8,128)(2,1)S(1)} %get-tuple-element.24), channel_id=1, source_target_pairs={{0,4},{4,8},{8,12},{1,5},{5,9},{9,13},{2,6},{6,10},{10,14},{3,7},{... | collective-permute-start | bytes 98312 | tf_op jit(solution)/shard_map/ppermute | solution.py:16
  118.2 34.6 %all-reduce = (f32[64]{0:T(128)S(1)}, f32[64]{0:T(128)S(1)}) all-reduce(f32[64]{0:T(128)S(1)} %get-tuple-element.37, f32[64]{0:T(128)S(1)} %get-tuple-element.39), channel_id=1, replica_groups=mesh['parts'=2,'tile'=4,'ch'=2,'sub'=2] {'tile','ch','sub'}, use_global_device_ids=true, to_apply=%region_2.5 | all-reduce | flops 128 | bytes 1024 | tf_op jit(solution)/shard_map/psum | solution.py:94
  152.9 0.5 broadcast_multiply_fusion.3
  153.4 0.5 broadcast_multiply_fusion.2
  154.0 1.3 collective-permute-start.15
  155.3 3.0 %collective-permute-start.14 = (bf16[64,4,1,128]{0,3,2,1:T(8,128)(2,1)S(1)}, bf16[64,4,1,128]{0,3,2,1:T(8,128)(2,1)S(1)}, u32[]{:S(2)}, u32[]{:S(2)}) collective-permute-start(bf16[64,4,1,128]{0,3,2,1:T(8,128)(2,1)S(1)} %get-tuple-element.16), channel_id=1, source_target_pairs={{0,1},{1,2},{2,3},{4,5},{5,6},{6,7},{8,9},{9,10},{10,11},{12,13},{... | collective-permute-start | bytes 196616 | tf_op jit(solution)/shard_map/ppermute | solution.py:16
  158.3 1.0 pad_maximum_fusion
  159.7 4.7 %gather_fusion.15 = bf16[2304,64]{1,0:T(8,128)(2,1)S(1)} fusion(bf16[64,2304]{0,1:T(8,128)(2,1)S(1)} %pad_maximum_fusion.5, s32[3072]{0:T(1024)S(1)} %pad_clamp_fusion), kind=kCustom, calls=%fused_computation.15.clone | custom fusion | bytes 599040 | tf_op jit(solution)/shard_map/jit(_take)/gather | solution.py:41
  164.3 4.7 %gather_fusion.14 = bf16[2304,64]{1,0:T(8,128)(2,1)S(1)} fusion(bf16[64,2304]{0,1:T(8,128)(2,1)S(1)} %pad_maximum_fusion.5, s32[3072]{0:T(1024)S(1)} %pad_clamp_fusion.1), kind=kCustom, calls=%fused_computation.14.clone | custom fusion | bytes 599040 | tf_op jit(solution)/shard_map/jit(_take)/gather | solution.py:41
  169.0 4.7 %gather_fusion.13 = bf16[2304,64]{1,0:T(8,128)(2,1)S(1)} fusion(bf16[64,2304]{0,1:T(8,128)(2,1)S(1)} %pad_maximum_fusion.5, s32[3072]{0:T(1024)S(1)} %pad_clamp_fusion.2), kind=kCustom, calls=%fused_computation.13.clone | custom fusion | bytes 599040 | tf_op jit(solution)/shard_map/jit(_take)/gather | solution.py:41
  174.9 0.9 fusion.17
  175.7 77.7 %all-reduce.4.cloned.1.call-done = (f32[27,64,64]{1,2,0:T(8,128)}, f32[27,64,64]{1,2,0:T(8,128)}) async-done(((f32[27,64,64]{1,2,0:T(8,128)}, f32[27,64,64]{1,2,0:T(8,128)}), (f32[27,64,64]{1,2,0:T(8,128)}, f32[27,64,64]{1,2,0:T(8,128)})) %all-reduce.4.cloned.1.call-update) | async-done | bytes 884752 | tf_op jit(solution)/shard_map/psum | solution.py:94
  253.5 1.3 broadcast_multiply_fusion.1
  254.7 1.2 copy.39
  256.0 1.2 copy.40
  (107 shorter events, 7.4 us)
Async XLA Ops:
  7.2 33.1 %copy-start = (bf16[27,64,64]{2,1,0:T(8,128)(2,1)S(1)}, bf16[27,64,64]{2,1,0:T(8,128)(2,1)}, u32[]{:S(2)}) copy-start(bf16[27,64,64]{2,1,0:T(8,128)(2,1)} %param.13) | copy-start | bytes 663556
  7.2 10.7 %copy-start.6 = (s32[1,1,27,256]{3,1,2,0:T(1,128)S(1)}, s32[1,1,27,256]{3,1,2,0:T(1,128)}, u32[]{:S(2)}) copy-start(s32[1,1,27,256]{3,1,2,0:T(1,128)} %param.18) | copy-start | bytes 82948
  7.2 246.3 %all-reduce.4.cloned.1.call-start = ((), (), s32[]{:S(2)}) async-start(), calls=%async_computation | async-start | bytes 3538944 | tf_op jit(solution)/shard_map/psum | solution.py:94
  11.0 7.4 %collective-permute-start.1 = (bf16[64,1,2,128]{0,3,2,1:T(8,128)(2,1)S(1)}, bf16[64,1,2,128]{0,3,2,1:T(8,128)(2,1)S(1)}, u32[]{:S(2)}, u32[]{:S(2)}) collective-permute-start(bf16[64,1,2,128]{0,3,2,1:T(8,128)(2,1)S(1)} %get-tuple-element.31), channel_id=1, source_target_pairs={{4,0},{8,4},{12,8},{5,1},{9,5},{13,9},{6,2},{10,6},{14,10},{7,3},{... | collective-permute-start | bytes 98312 | tf_op jit(solution)/shard_map/ppermute | solution.py:17
  12.3 7.5 %collective-permute-start = (bf16[64,1,2,128]{0,3,2,1:T(8,128)(2,1)S(1)}, bf16[64,1,2,128]{0,3,2,1:T(8,128)(2,1)S(1)}, u32[]{:S(2)}, u32[]{:S(2)}) collective-permute-start(bf16[64,1,2,128]{0,3,2,1:T(8,128)(2,1)S(1)} %get-tuple-element.30), channel_id=1, source_target_pairs={{0,4},{4,8},{8,12},{1,5},{5,9},{9,13},{2,6},{6,10},{10,14},{3,7},{... | collective-permute-start | bytes 98312 | tf_op jit(solution)/shard_map/ppermute | solution.py:16
  19.9 4.4 %collective-permute-start.3 = (bf16[64,4,1,128]{0,3,2,1:T(8,128)(2,1)S(1)}, bf16[64,4,1,128]{0,3,2,1:T(8,128)(2,1)S(1)}, u32[]{:S(2)}, u32[]{:S(2)}) collective-permute-start(bf16[64,4,1,128]{0,3,2,1:T(8,128)(2,1)S(1)} %get-tuple-element.23), channel_id=1, source_target_pairs={{1,0},{2,1},{3,2},{5,4},{6,5},{7,6},{9,8},{10,9},{11,10},{13,12},{... | collective-permute-start | bytes 196616 | tf_op jit(solution)/shard_map/ppermute | solution.py:17
  21.2 4.0 %collective-permute-start.2 = (bf16[64,4,1,128]{0,3,2,1:T(8,128)(2,1)S(1)}, bf16[64,4,1,128]{0,3,2,1:T(8,128)(2,1)S(1)}, u32[]{:S(2)}, u32[]{:S(2)}) collective-permute-start(bf16[64,4,1,128]{0,3,2,1:T(8,128)(2,1)S(1)} %get-tuple-element.22), channel_id=1, source_target_pairs={{0,1},{1,2},{2,3},{4,5},{5,6},{6,7},{8,9},{9,10},{10,11},{12,13},{... | collective-permute-start | bytes 196616 | tf_op jit(solution)/shard_map/ppermute | solution.py:16
  40.2 1.5 copy-start.1
  40.2 0.7 copy-start.8
  43.4 6.5 %collective-permute-start.5 = (bf16[64,1,2,128]{0,3,2,1:T(8,128)(2,1)S(1)}, bf16[64,1,2,128]{0,3,2,1:T(8,128)(2,1)S(1)}, u32[]{:S(2)}, u32[]{:S(2)}) collective-permute-start(bf16[64,1,2,128]{0,3,2,1:T(8,128)(2,1)S(1)} %get-tuple-element.29), channel_id=1, source_target_pairs={{4,0},{8,4},{12,8},{5,1},{9,5},{13,9},{6,2},{10,6},{14,10},{7,3},{... | collective-permute-start | bytes 98312 | tf_op jit(solution)/shard_map/ppermute | solution.py:17
  44.7 6.8 %collective-permute-start.4 = (bf16[64,1,2,128]{0,3,2,1:T(8,128)(2,1)S(1)}, bf16[64,1,2,128]{0,3,2,1:T(8,128)(2,1)S(1)}, u32[]{:S(2)}, u32[]{:S(2)}) collective-permute-start(bf16[64,1,2,128]{0,3,2,1:T(8,128)(2,1)S(1)} %get-tuple-element.28), channel_id=1, source_target_pairs={{0,4},{4,8},{8,12},{1,5},{5,9},{9,13},{2,6},{6,10},{10,14},{3,7},{... | collective-permute-start | bytes 98312 | tf_op jit(solution)/shard_map/ppermute | solution.py:16
  51.6 5.5 %collective-permute-start.7 = (bf16[64,4,1,128]{0,3,2,1:T(8,128)(2,1)S(1)}, bf16[64,4,1,128]{0,3,2,1:T(8,128)(2,1)S(1)}, u32[]{:S(2)}, u32[]{:S(2)}) collective-permute-start(bf16[64,4,1,128]{0,3,2,1:T(8,128)(2,1)S(1)} %get-tuple-element.21), channel_id=1, source_target_pairs={{1,0},{2,1},{3,2},{5,4},{6,5},{7,6},{9,8},{10,9},{11,10},{13,12},{... | collective-permute-start | bytes 196616 | tf_op jit(solution)/shard_map/ppermute | solution.py:17
  52.9 5.2 %collective-permute-start.6 = (bf16[64,4,1,128]{0,3,2,1:T(8,128)(2,1)S(1)}, bf16[64,4,1,128]{0,3,2,1:T(8,128)(2,1)S(1)}, u32[]{:S(2)}, u32[]{:S(2)}) collective-permute-start(bf16[64,4,1,128]{0,3,2,1:T(8,128)(2,1)S(1)} %get-tuple-element.20), channel_id=1, source_target_pairs={{0,1},{1,2},{2,3},{4,5},{5,6},{6,7},{8,9},{9,10},{10,11},{12,13},{... | collective-permute-start | bytes 196616 | tf_op jit(solution)/shard_map/ppermute | solution.py:16
  72.8 1.0 copy-start.4
  73.8 0.8 copy-start.5
  73.8 0.8 copy-start.7
  73.8 0.8 copy-start.9
  77.1 6.2 %collective-permute-start.9 = (bf16[64,1,2,128]{0,3,2,1:T(8,128)(2,1)S(1)}, bf16[64,1,2,128]{0,3,2,1:T(8,128)(2,1)S(1)}, u32[]{:S(2)}, u32[]{:S(2)}) collective-permute-start(bf16[64,1,2,128]{0,3,2,1:T(8,128)(2,1)S(1)} %get-tuple-element.27), channel_id=1, source_target_pairs={{4,0},{8,4},{12,8},{5,1},{9,5},{13,9},{6,2},{10,6},{14,10},{7,3},{... | collective-permute-start | bytes 98312 | tf_op jit(solution)/shard_map/ppermute | solution.py:17
  78.4 6.5 %collective-permute-start.8 = (bf16[64,1,2,128]{0,3,2,1:T(8,128)(2,1)S(1)}, bf16[64,1,2,128]{0,3,2,1:T(8,128)(2,1)S(1)}, u32[]{:S(2)}, u32[]{:S(2)}) collective-permute-start(bf16[64,1,2,128]{0,3,2,1:T(8,128)(2,1)S(1)} %get-tuple-element.26), channel_id=1, source_target_pairs={{0,4},{4,8},{8,12},{1,5},{5,9},{9,13},{2,6},{6,10},{10,14},{3,7},{... | collective-permute-start | bytes 98312 | tf_op jit(solution)/shard_map/ppermute | solution.py:16
  85.0 8.7 %collective-permute-start.11 = (bf16[64,4,1,128]{0,3,2,1:T(8,128)(2,1)S(1)}, bf16[64,4,1,128]{0,3,2,1:T(8,128)(2,1)S(1)}, u32[]{:S(2)}, u32[]{:S(2)}) collective-permute-start(bf16[64,4,1,128]{0,3,2,1:T(8,128)(2,1)S(1)} %get-tuple-element.19), channel_id=1, source_target_pairs={{1,0},{2,1},{3,2},{5,4},{6,5},{7,6},{9,8},{10,9},{11,10},{13,12},{... | collective-permute-start | bytes 196616 | tf_op jit(solution)/shard_map/ppermute | solution.py:17
  86.3 7.4 %collective-permute-start.10 = (bf16[64,4,1,128]{0,3,2,1:T(8,128)(2,1)S(1)}, bf16[64,4,1,128]{0,3,2,1:T(8,128)(2,1)S(1)}, u32[]{:S(2)}, u32[]{:S(2)}) collective-permute-start(bf16[64,4,1,128]{0,3,2,1:T(8,128)(2,1)S(1)} %get-tuple-element.18), channel_id=1, source_target_pairs={{0,1},{1,2},{2,3},{4,5},{5,6},{6,7},{8,9},{9,10},{10,11},{12,13},{... | collective-permute-start | bytes 196616 | tf_op jit(solution)/shard_map/ppermute | solution.py:16
  108.7 0.8 copy-start.10
  109.0 1.1 copy-start.2
  112.3 41.6 %collective-permute-start.13 = (bf16[64,1,2,128]{0,3,2,1:T(8,128)(2,1)S(1)}, bf16[64,1,2,128]{0,3,2,1:T(8,128)(2,1)S(1)}, u32[]{:S(2)}, u32[]{:S(2)}) collective-permute-start(bf16[64,1,2,128]{0,3,2,1:T(8,128)(2,1)S(1)} %get-tuple-element.25), channel_id=1, source_target_pairs={{4,0},{8,4},{12,8},{5,1},{9,5},{13,9},{6,2},{10,6},{14,10},{7,3},{... | collective-permute-start | bytes 98312 | tf_op jit(solution)/shard_map/ppermute | solution.py:17
  113.6 40.3 %collective-permute-start.12 = (bf16[64,1,2,128]{0,3,2,1:T(8,128)(2,1)S(1)}, bf16[64,1,2,128]{0,3,2,1:T(8,128)(2,1)S(1)}, u32[]{:S(2)}, u32[]{:S(2)}) collective-permute-start(bf16[64,1,2,128]{0,3,2,1:T(8,128)(2,1)S(1)} %get-tuple-element.24), channel_id=1, source_target_pairs={{0,4},{4,8},{8,12},{1,5},{5,9},{9,13},{2,6},{6,10},{10,14},{3,7},{... | collective-permute-start | bytes 98312 | tf_op jit(solution)/shard_map/ppermute | solution.py:16
  154.0 5.4 %collective-permute-start.15 = (bf16[64,4,1,128]{0,3,2,1:T(8,128)(2,1)S(1)}, bf16[64,4,1,128]{0,3,2,1:T(8,128)(2,1)S(1)}, u32[]{:S(2)}, u32[]{:S(2)}) collective-permute-start(bf16[64,4,1,128]{0,3,2,1:T(8,128)(2,1)S(1)} %get-tuple-element.17), channel_id=1, source_target_pairs={{1,0},{2,1},{3,2},{5,4},{6,5},{7,6},{9,8},{10,9},{11,10},{13,12},{... | collective-permute-start | bytes 196616 | tf_op jit(solution)/shard_map/ppermute | solution.py:17
  155.3 4.1 %collective-permute-start.14 = (bf16[64,4,1,128]{0,3,2,1:T(8,128)(2,1)S(1)}, bf16[64,4,1,128]{0,3,2,1:T(8,128)(2,1)S(1)}, u32[]{:S(2)}, u32[]{:S(2)}) collective-permute-start(bf16[64,4,1,128]{0,3,2,1:T(8,128)(2,1)S(1)} %get-tuple-element.16), channel_id=1, source_target_pairs={{0,1},{1,2},{2,3},{4,5},{5,6},{6,7},{8,9},{9,10},{10,11},{12,13},{... | collective-permute-start | bytes 196616 | tf_op jit(solution)/shard_map/ppermute | solution.py:16
  254.7 1.2 copy-start.3
Sparse Core Ops, SparseCore 0:
  159.5 93.9 all-reduce.3
where the time goes:
time: 265 us; the launch traced here: 264 us
  waiting for transfers between devices  84.4 us (32%)
  local copies, waits for them, and re-layouts  69.9 us (26%)
  starting transfers between devices  46.7 us (18%)
  blocking collectives  34.6 us (13%)
  between operations  15 us (6%)
  other arithmetic  7.72 us (3%)
  matrix products  5.69 us (2%)
    psum x1, waiting for transfers between devices, per_device(): lax.psum((grad_w1, grad_b1, grad_w2, grad_b2), ('tile', 'ch', 'sub'))  77.7 us
    gather x24, local copies, waits for them, and re-layouts, gather_offsets(): jnp.take(framed, near_rows[9 * k:9 * k + 9], axis=1, mode='fill', fill_va...  58.8 us
    ppermute x8, starting transfers between devices, padded(): before = lax.ppermute(last, axis, up)  36.3 us
    psum x1, blocking collectives, per_device(): lax.psum((grad_w1, grad_b1, grad_w2, grad_b2), ('tile', 'ch', 'sub'))  34.6 us
    ppermute x8, starting transfers between devices, padded(): after = lax.ppermute(initial, axis, down)  10.3 us
    ppermute x8, waiting for transfers between devices, padded(): before = lax.ppermute(last, axis, up)  6.35 us
  transfers between devices with their start and end apart: 17, of which 7 were waited for; matrix products, arithmetic and copies ran while one was open for 8% of the time, Pallas kernels for 0%

commit v1 on v0

v1 whole, which is shorter than its diff:
```python
import functools
import math

import jax
import jax.numpy as jnp
from jax import lax
from jax.experimental import pallas as pl
from jax.experimental.pallas import tpu as pltpu
from jax.sharding import PartitionSpec as P

BF = jnp.bfloat16
F32 = jnp.float32
MESH = pl.DeviceIdType.MESH
SLOT = 32
PAIRS = 16
OFFS = 27
RING = [(p, q) for p in range(4) for q in range(4) if not (p in (1, 2) and q in (1, 2))]
SHIFT = (-1, 0, 0, 1)
HALF = (1, 0, 1, 0)


def dot(a, b, dims=((1,), (0,))):
    return lax.dot_general(a, b, (dims, ((), ())), preferred_element_type=F32)


def silu_slope(values):
    sigmoid = jax.nn.sigmoid(values)
    return sigmoid * (1.0 + values * (1.0 - sigmoid))


def kernel(
    tiles, chs, subs, scale,
    feats, w1, b1, w2, b2, cot, nbr, shell,
    gf_out, gw1_out, gb1_out, gw2_out, gb2_out,
    onehot, frames, pick_a, pick_b, pick_c, wf1, wf2, wt1, wt2, bucket_sel, buckets, table,
    part, rs1, mid, rs2, full,
    halo_send, halo_recv, s1, r1, s2, r2, s3, r3, s4, r4,
):
    vox = feats.shape[1]
    chan = feats.shape[0]
    tys = chs * subs
    tx = lax.axis_index("tile")
    ty = lax.axis_index("ch") * subs + lax.axis_index("sub")
    quarter = PAIRS * chan // tys
    chunk = max(16, quarter // tiles)
    owners = quarter // chunk
    width = OFFS * chan

    def device(x, y):
        return {"tile": x, "ch": y // subs, "sub": y % subs}

    def exists(dx, dy):
        ok = None
        for at, d, n in ((tx, dx, tiles), (ty, dy, tys)):
            if d:
                here = at > 0 if d < 0 else at < n - 1
                ok = here if ok is None else jnp.logical_and(ok, here)
        return ok

    for stage in range(4):
        frames[stage, vox:, :] = jnp.zeros((16 * SLOT, 2 * chan), BF)

    barrier = pltpu.get_barrier_semaphore()
    for dx in (-1, 0, 1):
        for dy in (-1, 0, 1):
            if dx or dy:

                @pl.when(exists(dx, dy))
                def _():
                    pl.semaphore_signal(
                        barrier, inc=1, device_id=device(tx + dx, ty + dy), device_id_type=MESH
                    )

    for d in range(1, tys):
        pl.semaphore_signal(
            barrier, inc=1, device_id=device(tx, lax.rem(ty + d, tys)), device_id_type=MESH
        )
    for d in range(1, tiles):
        pl.semaphore_signal(
            barrier, inc=1, device_id=device(lax.rem(tx + d, tiles), ty), device_id_type=MESH
        )
    near_x = 1 + jnp.minimum(tx, 1) + jnp.minimum(tiles - 1 - tx, 1)
    near_y = 1 + jnp.minimum(ty, 1) + jnp.minimum(tys - 1 - ty, 1)

    def halo_copy(stage, p, q):
        quad = 2 * HALF[p] + HALF[q]
        return pltpu.make_async_remote_copy(
            src_ref=buckets.at[stage, pl.ds(quad * SLOT, SLOT)],
            dst_ref=frames.at[stage, pl.ds(vox + (4 * p + q) * SLOT, SLOT)],
            send_sem=halo_send.at[stage, 4 * p + q],
            recv_sem=halo_recv.at[stage, 4 * p + q],
            device_id=device(tx - SHIFT[p], ty - SHIFT[q]),
            device_id_type=MESH,
        )

    def send_halo(stage, own):
        frames[stage, :vox, :] = own
        cut = dot(bucket_sel[...], own).astype(BF)
        buckets[stage] = cut
        for p, q in RING:

            @pl.when(exists(-SHIFT[p], -SHIFT[q]))
            def _():
                halo_copy(stage, p, q).start()

        for a in range(2):
            for b in range(2):
                base = vox + (4 * (1 + a) + 1 + b) * SLOT
                quad = 2 * a + b
                frames[stage, base : base + SLOT, :] = cut[quad * SLOT : (quad + 1) * SLOT]

    def wait_halo(stage):
        for p, q in RING:

            @pl.when(exists(SHIFT[p], SHIFT[q]))
            def _():
                halo_copy(stage, p, q).wait_recv()

    def wait_sent(stage):
        for p, q in RING:

            @pl.when(exists(-SHIFT[p], -SHIFT[q]))
            def _():
                halo_copy(stage, p, q).wait_send()

    low = lax.broadcasted_iota(jnp.int32, (vox, 2 * chan), 1) < chan

    def pick(stage, into, flip):
        def pair(j, _):
            k0 = 26 - 2 * j if flip else 2 * j
            k1 = 25 - 2 * j if flip else 2 * j + 1
            framed = frames[stage]
            first = dot(onehot[k0], framed)
            second = dot(onehot[k1], framed)
            at = pl.multiple_of(j * 2 * chan, 2 * chan)
            into[:, pl.ds(at, 2 * chan)] = jnp.where(low, first, second).astype(BF)
            return 0

        lax.fori_loop(0, OFFS // 2, pair, 0)
        last = dot(onehot[0 if flip else 26], frames[stage])
        into[:, width - chan :] = jnp.where(low, last, 1.0).astype(BF)

    quads = [shell[a, b : b + 1, :][:, :SLOT] for a in range(2) for b in range(2)]
    listed = jnp.concatenate(quads, axis=1)
    by_voxel = lax.broadcasted_iota(jnp.int32, (vox, 4 * SLOT), 0) == listed
    bucket_sel[...] = jnp.where(by_voxel, 1.0, 0.0).T.astype(BF)

    both = feats[...].astype(F32)
    inputs = jnp.concatenate([both, both], axis=0).T
    pl.semaphore_wait(barrier, near_x * near_y - 1 + (tys - 1) + (tiles - 1))
    send_halo(0, inputs.astype(BF))

    index = nbr[...]
    outer = index - vox
    slot = jnp.bitwise_and(outer, 127)
    packed = vox + lax.shift_right_logical(outer, 7) * SLOT + slot
    known = jnp.logical_and(index < vox + 16 * 128, slot < SLOT)
    packed = jnp.where(index < vox, index, jnp.where(known, packed, -1))
    table[...] = jnp.concatenate(
        [packed, jnp.zeros((128 - OFFS, vox), jnp.int32)], axis=0
    ).T
    columns = vox + 16 * SLOT
    block = 32

    def build(i, _):
        rows = pl.ds(pl.multiple_of(i * block, block), block)
        entries = table[rows, :]
        lanes = lax.broadcasted_iota(jnp.int32, (block, columns), 1)
        for k in range(OFFS):
            hit = entries[:, k : k + 1] == lanes
            onehot[k, rows, :] = jnp.where(hit, 1.0, 0.0).astype(BF)
        return 0

    lax.fori_loop(0, vox // block, build, 0)

    for weight, forward, turned in ((w1, wf1, wt1), (w2, wf2, wt2)):
        for k in range(OFFS):
            value = weight[k]
            forward[k * chan : (k + 1) * chan, :] = jnp.concatenate([value, value], axis=1)
        forward[width:, :] = jnp.zeros((chan, 2 * chan), BF)
        for j in range(PAIRS - 2):
            left = weight[2 * j]
            right = weight[2 * j + 1] if 2 * j + 1 < OFFS else jnp.zeros((chan, chan), BF)
            beside = jnp.concatenate([left, right], axis=1)
            turned[:chan, 2 * chan * j : 2 * chan * (j + 1)] = beside
            turned[chan:, 2 * chan * j : 2 * chan * (j + 1)] = beside

    def twice(bias):
        return jnp.concatenate([bias[...], bias[...]], axis=1)

    def ty_copy(g, d):
        to = lax.rem(ty + d, tys)
        return pltpu.make_async_remote_copy(
            src_ref=part.at[g, pl.ds(pl.multiple_of(to * quarter, quarter), quarter)],
            dst_ref=rs1.at[g, d],
            send_sem=s1.at[g, d],
            recv_sem=r1.at[g, d],
            device_id=device(tx, to),
            device_id_type=MESH,
        )

    def tile_copy(g, d):
        to = lax.rem(tx + d, tiles)
        at = pl.multiple_of(lax.rem(to, owners) * chunk, chunk)
        return pltpu.make_async_remote_copy(
            src_ref=mid.at[g, pl.ds(at, chunk)],
            dst_ref=rs2.at[g, d],
            send_sem=s2.at[g, d],
            recv_sem=r2.at[g, d],
            device_id=device(to, ty),
            device_id_type=MESH,
        )

    def chunk_rows(x):
        return pl.ds(pl.multiple_of(ty * quarter + lax.rem(x, owners) * chunk, chunk), chunk)

    def back_tile(g, d, x):
        return pltpu.make_async_remote_copy(
            src_ref=full.at[g, chunk_rows(x)],
            dst_ref=full.at[g, chunk_rows(x)],
            send_sem=s3.at[g, d],
            recv_sem=r3.at[g, d],
            device_id=device(lax.rem(tx + d, tiles), ty),
            device_id_type=MESH,
        )

    def back_ty(g, d, y):
        rows = pl.ds(pl.multiple_of(y * quarter, quarter), quarter)
        return pltpu.make_async_remote_copy(
            src_ref=full.at[g, rows],
            dst_ref=full.at[g, rows],
            send_sem=s4.at[g, d],
            recv_sem=r4.at[g, d],
            device_id=device(tx, lax.rem(ty + d, tys)),
            device_id_type=MESH,
        )

    def owned(x, body):
        if owners >= tiles:
            body()
        else:
            pl.when(x < owners)(body)

    def reduce_start(g, gradient, picked):
        turned = gradient.T[:chan].astype(BF)
        terms = dot(turned, picked[...])
        for j in range(PAIRS - 2):
            part[g, j * chan : (j + 1) * chan, :] = terms[
                :, 2 * chan * j : 2 * chan * (j + 1)
            ].astype(BF)
        part[g, (PAIRS - 2) * chan :, :] = jnp.zeros((2 * chan, 2 * chan), BF)
        for d in range(1, tys):
            ty_copy(g, d).start()

    def reduce_tiles(g):
        for d in range(1, tys):
            ty_copy(g, d).wait_recv()
        own = pl.ds(pl.multiple_of(ty * quarter, quarter), quarter)
        total = part[g, own, :].astype(F32)
        for d in range(1, tys):
            total = total + rs1[g, d].astype(F32)
        for j in range(quarter // chan):
            flat = total[j * chan : (j + 1) * chan].T
            mid[g, j * chan : (j + 1) * chan, :] = jnp.concatenate(
                [flat[:chan], flat[chan:]], axis=1
            ).astype(BF)
        for d in range(1, tiles):
            owned(lax.rem(tx + d, tiles), lambda: tile_copy(g, d).start())

    def spread_tiles(g):
        def body():
            for d in range(1, tiles):
                tile_copy(g, d).wait_recv()
            at = pl.multiple_of(lax.rem(tx, owners) * chunk, chunk)
            total = mid[g, pl.ds(at, chunk), :].astype(F32)
            for d in range(1, tiles):
                total = total + rs2[g, d].astype(F32)
            full[g, chunk_rows(tx), :] = total.astype(BF)
            for d in range(1, tiles):
                back_tile(g, d, tx).start()

        owned(tx, body)

    def spread_ty(g):
        for d in range(1, tiles):
            source = lax.rem(tx - d + tiles, tiles)
            owned(source, lambda: back_tile(g, d, source).wait_recv())
        for d in range(1, tys):
            back_ty(g, d, ty).start()

    def finish(g, gw_out, gb_out):
        for d in range(1, tys):
            back_ty(g, d, lax.rem(ty - d + tys, tys)).wait_recv()
        for j in range(PAIRS - 2):
            value = full[g, j * chan : (j + 1) * chan, :].astype(F32) * scale
            gw_out[2 * j] = value[:, :chan]
            if 2 * j + 1 < OFFS:
                gw_out[2 * j + 1] = value[:, chan:]
            else:
                gb_out[...] = value[:1, chan:]

    def drain(g):
        for d in range(1, tys):
            ty_copy(g, d).wait_send()
            back_ty(g, d, ty).wait_send()
        for d in range(1, tiles):
            owned(lax.rem(tx + d, tiles), lambda: tile_copy(g, d).wait_send())
            owned(tx, lambda: back_tile(g, d, tx).wait_send())

    wait_halo(0)
    pick(0, pick_a, False)
    first = dot(pick_a[...], wf1[...]) + twice(b1)
    hidden = (first * jax.nn.sigmoid(first)).astype(BF)
    send_halo(1, hidden)
    upstream = cot[...].astype(F32)
    upstream = jnp.concatenate([upstream, upstream], axis=0).T
    wait_halo(1)
    pick(1, pick_b, False)
    second = dot(pick_b[...], wf2[...]) + twice(b2)
    grad_out = (upstream * silu_slope(inputs + second)).astype(BF)

    send_halo(2, grad_out)
    grad_out = grad_out.astype(F32)
    reduce_start(1, grad_out, pick_b)
    wait_halo(2)
    pick(2, pick_c, True)
    back = dot(pick_c[...], wt2[...], ((1,), (1,)))
    grad_pre = (back * silu_slope(first)).astype(BF)
    send_halo(3, grad_pre)
    reduce_start(0, grad_pre.astype(F32), pick_a)
    reduce_tiles(1)
    wait_halo(3)
    pick(3, pick_c, True)
    reduce_tiles(0)
    spread_tiles(1)
    back = dot(pick_c[...], wt1[...], ((1,), (1,)))
    gf_out[...] = (grad_out + back).T[:chan]
    spread_tiles(0)
    spread_ty(1)
    spread_ty(0)
    finish(1, gw2_out, gb2_out)
    finish(0, gw1_out, gb1_out)
    for stage in range(4):
        wait_sent(stage)
    drain(1)
    drain(0)


def per_device(feats, weight1, bias1, weight2, bias2, cotangent, neighbors, shell):
    tiles, chs, subs = (lax.axis_size(a) for a in ("tile", "ch", "sub"))
    chan, vox = feats.shape[2:]
    tys = chs * subs
    scale = 1.0 / math.sqrt(vox * tiles * tys)
    columns = vox + 16 * SLOT
    rows = PAIRS * chan
    quarter = rows // tys
    chunk = max(16, quarter // tiles)
    wide = (PAIRS - 2) * 2 * chan
    lanes = 2 * chan
    vmem = pl.BlockSpec(memory_space=pltpu.VMEM)
    dma = pltpu.SemaphoreType.DMA
    gf, gw1, gb1, gw2, gb2 = pl.pallas_call(
        functools.partial(kernel, tiles, chs, subs, scale),
        out_shape=(
            jax.ShapeDtypeStruct((chan, vox), F32),
            jax.ShapeDtypeStruct((OFFS, chan, chan), F32),
            jax.ShapeDtypeStruct((1, chan), F32),
            jax.ShapeDtypeStruct((OFFS, chan, chan), F32),
            jax.ShapeDtypeStruct((1, chan), F32),
        ),
        in_specs=[vmem] * 8,
        out_specs=(vmem,) * 5,
        scratch_shapes=[
            pltpu.VMEM((OFFS, vox, columns), BF),
            pltpu.VMEM((4, columns, lanes), BF),
            pltpu.VMEM((vox, wide), BF),
            pltpu.VMEM((vox, wide), BF),
            pltpu.VMEM((vox, wide), BF),
            pltpu.VMEM((wide, lanes), BF),
            pltpu.VMEM((wide, lanes), BF),
            pltpu.VMEM((lanes, wide), BF),
            pltpu.VMEM((lanes, wide), BF),
            pltpu.VMEM((4 * SLOT, vox), BF),
            pltpu.VMEM((4, 4 * SLOT, lanes), BF),
            pltpu.VMEM((vox, 128), jnp.int32),
            pltpu.VMEM((2, rows, lanes), BF),
            pltpu.VMEM((2, tys, quarter, lanes), BF),
            pltpu.VMEM((2, quarter, lanes), BF),
            pltpu.VMEM((2, tiles, chunk, lanes), BF),
            pltpu.VMEM((2, rows, lanes), BF),
            dma((4, 16)),
            dma((4, 16)),
            dma((2, tys)),
            dma((2, tys)),
            dma((2, tiles)),
            dma((2, tiles)),
            dma((2, tiles)),
            dma((2, tiles)),
            dma((2, tys)),
            dma((2, tys)),
        ],
        compiler_params=pltpu.CompilerParams(
            collective_id=0, has_side_effects=True, vmem_limit_bytes=48 * 1024 * 1024
        ),
    )(
        feats[0, 0], weight1, bias1[None], weight2, bias2[None], cotangent[0, 0],
        neighbors[0, 0], shell[0, 0],
    )
    return gf[None, None], gw1, gb1[0], gw2, gb2[0]


def solution(mesh):
    placed = (
        P(("parts", "tile"), ("ch", "sub"), None, None),
        P(),
        P(),
        P(),
        P(),
        P(("parts", "tile"), ("ch", "sub"), None, None),
        P(("parts", "tile"), ("ch", "sub"), None, None),
        P(("parts", "tile"), ("ch", "sub"), None, None, None),
    )
    return jax.shard_map(
        per_device,
        mesh=mesh,
        in_specs=placed,
        out_specs=(
            P(("parts", "tile"), ("ch", "sub"), None, None),
            P("parts", None, None),
            P("parts"),
            P("parts", None, None),
            P("parts"),
        ),
        check_vma=False,
    )
```

time: 265 us -> 59.9 us (0.23)
  waiting for transfers between devices: 84.4 us -> 0 us
  local copies, waits for them, and re-layouts: 69.9 us -> 6.92 us
  Pallas kernels: 0 us -> 52 us
  starting transfers between devices: 46.7 us -> 0 us
  blocking collectives: 34.6 us -> 0 us
  between operations: 15 us -> 0.7 us
  other arithmetic: 7.72 us -> 0 us
  matrix products: 5.69 us -> 0 us
    psum x1 -> x0, waiting for transfers between devices: 77.7 us -> none  [per_device(): lax.psum((grad_w1, grad_b1, grad_w2, grad_b2), ('tile', 'ch', 'sub'))]
    gather x28 -> x0, local copies, waits for them, and re-layouts: 64.2 us -> none  [the longest x24 58.8 us: gather_offsets(): jnp.take(framed, near_rows[9 * k:9 * k + 9], axis=1, mode='fill', fill_va...]
    pallas_call x0 -> x1, Pallas kernels: none -> 52 us  [per_device(): pl.pallas_call(functools.partial(kernel, tiles, chs, subs, scale), out_sh...]
    ppermute x16 -> x0, starting transfers between devices: 46.7 us -> none  [the longest x8 36.3 us: padded(): before = lax.ppermute(last, axis, up)]
    psum x1 -> x0, blocking collectives: 34.6 us -> none  [per_device(): lax.psum((grad_w1, grad_b1, grad_w2, grad_b2), ('tile', 'ch', 'sub'))]
    ppermute x16 -> x0, waiting for transfers between devices: 6.68 us -> none  [the longest x8 6.35 us: padded(): before = lax.ppermute(last, axis, up)]
    dot_general x18 -> x0, matrix products: 5.69 us -> none  [the longest x12 4.11 us: convolve_picked(): jnp.einsum('kio,ikr->or', weight[9 * k:9 * k + 9], picked_blocks[k], pref...]
    concatenate x14 -> x0, other arithmetic: 3.27 us -> none  [the longest x2 2.02 us: weight_grad(): return jnp.concatenate(pieces, axis=0)]
  transfers between devices with their start and end apart: 17 -> 0, of which waited for: 7 -> 0; matrix products, arithmetic and copies ran while one was open for 8% -> 0% of each run, Pallas kernels for 0% -> 0%
where the time goes in v1:
time: 59.9 us; the launch traced here: 59.7 us
  Pallas kernels  52 us (87%)
  local copies, waits for them, and re-layouts  6.92 us (12%)
  between operations  0.7 us (1%)
    pallas_call x1, Pallas kernels, per_device(): pl.pallas_call(functools.partial(kernel, tiles, chs, subs, scale), out_sh...  52 us
    unnamed x20, local copies, waits for them, and re-layouts  6.92 us

profile of v1, /device:TPU:0, one launch (start us, length us, event | category | flops | bytes accessed | tf_op | source)
XLA Modules:
  0.0 59.7 jit_solution(17411391811521832214)
XLA Ops:
  0.6 0.0 copy-start.6
  0.6 0.0 copy-start.4
  0.7 0.0 copy-start.2
  0.7 0.0 copy-start.3
  0.7 0.8 %copy.15 = s32[1,1,27,256]{3,2,1,0:T(8,128)S(1)} copy(s32[1,1,27,256]{3,1,2,0:T(1,128)} %param.14) | data formatting | bytes 55296
  1.4 0.0 copy-start.5
  1.4 0.0 copy-done.6
  1.4 0.0 copy-done.4
  1.5 0.0 copy-done.2
  1.5 0.0 copy-done.3
  1.5 0.6 %copy-done.5 = f32[64]{0:T(128)S(1)} copy-done((f32[64]{0:T(128)S(1)}, f32[64]{0:T(128)}, u32[]{:S(2)}) %copy-start.5) | copy-done | bytes 280
  2.1 0.0 copy-start
  2.1 1.0 %copy-done = bf16[27,64,64]{2,1,0:T(8,128)(2,1)S(1)} copy-done((bf16[27,64,64]{2,1,0:T(8,128)(2,1)S(1)}, bf16[27,64,64]{2,1,0:T(8,128)(2,1)}, u32[]{:S(2)}) %copy-start) | copy-done | bytes 221208
  3.1 0.0 copy-start.1
  3.1 1.0 %copy-done.1 = bf16[27,64,64]{2,1,0:T(8,128)(2,1)S(1)} copy-done((bf16[27,64,64]{2,1,0:T(8,128)(2,1)S(1)}, bf16[27,64,64]{2,1,0:T(8,128)(2,1)}, u32[]{:S(2)}) %copy-start.1) | copy-done | bytes 221208
  4.1 52.0 %shard_map.119 = (f32[64,256]{1,0:T(8,128)S(1)}, f32[27,64,64]{2,1,0:T(8,128)S(1)}, f32[1,64]{1,0:T(1,128)S(1)}, f32[27,64,64]{2,1,0:T(8,128)S(1)}, f32[1,64]{1,0:T(1,128)S(1)}) custom-call(bf16[64,256]{1,0:T(8,128)(2,1)S(1)} %bitcast.13, bf16[27,64,64]{2,1,0:T(8,128)(2,1)S(1)} %copy-done, f32[1,64]{1,0:T(1,128)S(1)} %bitcast.16, ...), custom_call_target="tpu_custom_call" | custom-call | tf_op jit(solution)/shard_map/pallas_call | solution.py:362
  56.2 0.6 %copy.21 = f32[1,1,64,256]{3,2,1,0:T(8,128)} copy(f32[1,1,64,256]{3,2,1,0:T(8,128)S(1)} %bitcast.12) | data formatting | bytes 131072
  56.8 0.9 %copy.22 = f32[27,64,64]{2,1,0:T(8,128)} copy(f32[27,64,64]{2,1,0:T(8,128)S(1)} %get-tuple-element.21) | data formatting | bytes 884736
  57.7 0.5 copy.23
  58.2 0.9 %copy.24 = f32[27,64,64]{2,1,0:T(8,128)} copy(f32[27,64,64]{2,1,0:T(8,128)S(1)} %get-tuple-element.23) | data formatting | bytes 884736
  59.1 0.5 copy.25
Async XLA Ops:
  0.6 0.8 %copy-start.6 = (f32[64]{0:T(128)S(1)}, f32[64]{0:T(128)}, u32[]{:S(2)}) copy-start(f32[64]{0:T(128)} %param.12) | copy-start | bytes 772
  0.6 0.8 %copy-start.4 = (s32[1,1,2,2,128]{4,3,2,1,0:T(2,128)S(1)}, s32[1,1,2,2,128]{4,3,2,1,0:T(2,128)}, u32[]{:S(2)}) copy-start(s32[1,1,2,2,128]{4,3,2,1,0:T(2,128)} %param.15) | copy-start | bytes 6148
  0.7 0.8 %copy-start.2 = (bf16[1,1,64,256]{3,2,1,0:T(8,128)(2,1)S(1)}, bf16[1,1,64,256]{3,2,1,0:T(8,128)(2,1)}, u32[]{:S(2)}) copy-start(bf16[1,1,64,256]{3,2,1,0:T(8,128)(2,1)} %param.8) | copy-start | bytes 98308
  0.7 0.8 %copy-start.3 = (bf16[1,1,64,256]{3,2,1,0:T(8,128)(2,1)S(1)}, bf16[1,1,64,256]{3,2,1,0:T(8,128)(2,1)}, u32[]{:S(2)}) copy-start(bf16[1,1,64,256]{3,2,1,0:T(8,128)(2,1)} %param.13) | copy-start | bytes 98308
  1.4 0.7 %copy-start.5 = (f32[64]{0:T(128)S(1)}, f32[64]{0:T(128)}, u32[]{:S(2)}) copy-start(f32[64]{0:T(128)} %param.10) | copy-start | bytes 772
  2.1 1.0 %copy-start = (bf16[27,64,64]{2,1,0:T(8,128)(2,1)S(1)}, bf16[27,64,64]{2,1,0:T(8,128)(2,1)}, u32[]{:S(2)}) copy-start(bf16[27,64,64]{2,1,0:T(8,128)(2,1)} %w1.1) | copy-start | bytes 663556
  3.1 1.0 %copy-start.1 = (bf16[27,64,64]{2,1,0:T(8,128)(2,1)S(1)}, bf16[27,64,64]{2,1,0:T(8,128)(2,1)}, u32[]{:S(2)}) copy-start(bf16[27,64,64]{2,1,0:T(8,128)(2,1)} %w2.1) | copy-start | bytes 663556

commit v2 on v1

v2 whole, which is shorter than its diff:
```python
import functools
import math

import jax
import jax.numpy as jnp
from jax import lax
from jax.experimental import pallas as pl
from jax.experimental.pallas import tpu as pltpu
from jax.sharding import PartitionSpec as P

BF = jnp.bfloat16
F32 = jnp.float32
MESH = pl.DeviceIdType.MESH
SLOT = 32
PAIRS = 16
OFFS = 27
UNROLL = 7
RING = [
    (0, 0), (0, 1), (0, 2), (0, 3), (1, 3), (2, 3),
    (3, 3), (3, 2), (3, 1), (3, 0), (2, 0), (1, 0),
]
BESIDE = 5
FIRST = (10, 1, 7, 4)
SHIFT = (-1, 0, 0, 1)
HALF = (1, 0, 1, 0)


def dot(a, b, dims=((1,), (0,))):
    return lax.dot_general(a, b, (dims, ((), ())), preferred_element_type=F32)


def silu_slope(values):
    sigmoid = jax.nn.sigmoid(values)
    return sigmoid * (1.0 + values * (1.0 - sigmoid))


def kernel(
    tiles, chs, subs,
    feats_in, w1_in, b1, w2_in, b2, cot_in, nbr_in, shell_in,
    gf_out, full_out,
    feats, w1, w2, cot, nbr, shell, in_sem,
    own_hot, halo_hot, ring, own_a, own_b, own_c, halo_a, halo_b, halo_c,
    wf1, wf2, wt1, wt2, gather_sel, scatter_sel, buckets, table,
    part, rs1, mid, rs2, full,
    halo_send, halo_recv, s1, r1, s2, r2, s3, r3, s4, r4,
):
    vox = feats.shape[1]
    chan = feats.shape[0]
    lanes = 2 * chan
    width = OFFS * chan
    tys = chs * subs
    tx = lax.axis_index("tile")
    ty = lax.axis_index("ch") * subs + lax.axis_index("sub")
    quarter = PAIRS * chan // tys
    chunk = max(chan, quarter // tiles)
    owners = quarter // chunk

    loads = [
        pltpu.make_async_copy(src, dst, in_sem.at[i])
        for i, (src, dst) in enumerate((
            (feats_in.at[0, 0], feats),
            (shell_in.at[0, 0], shell),
            (nbr_in.at[0, 0], nbr),
            (w1_in, w1),
            (cot_in.at[0, 0], cot),
            (w2_in, w2),
        ))
    ]
    for load in loads:
        load.start()

    def device(x, y):
        return {"tile": x, "ch": y // subs, "sub": y % subs}

    def exists(dx, dy):
        ok = None
        for at, d, n in ((tx, dx, tiles), (ty, dy, tys)):
            if d:
                here = at > 0 if d < 0 else at < n - 1
                ok = here if ok is None else jnp.logical_and(ok, here)
        return ok

    for stage in range(4):
        ring[stage] = jnp.zeros(ring.shape[1:], BF)

    barrier = pltpu.get_barrier_semaphore()
    for dx in (-1, 0, 1):
        for dy in (-1, 0, 1):
            if dx or dy:

                @pl.when(exists(dx, dy))
                def _():
                    pl.semaphore_signal(
                        barrier, inc=1, device_id=device(tx + dx, ty + dy), device_id_type=MESH
                    )

    for d in range(1, tys):
        pl.semaphore_signal(
            barrier, inc=1, device_id=device(tx, lax.rem(ty + d, tys)), device_id_type=MESH
        )
    for d in range(1, tiles):
        pl.semaphore_signal(
            barrier, inc=1, device_id=device(lax.rem(tx + d, tiles), ty), device_id_type=MESH
        )
    near_x = 1 + jnp.minimum(tx, 1) + jnp.minimum(tiles - 1 - tx, 1)
    near_y = 1 + jnp.minimum(ty, 1) + jnp.minimum(tys - 1 - ty, 1)

    def halo_copy(stage, n):
        p, q = RING[n]
        quad = 2 * HALF[p] + HALF[q]
        return pltpu.make_async_remote_copy(
            src_ref=buckets.at[stage, pl.ds(quad * SLOT, SLOT)],
            dst_ref=ring.at[stage, pl.ds(n * SLOT, SLOT)],
            send_sem=halo_send.at[stage, n],
            recv_sem=halo_recv.at[stage, n],
            device_id=device(tx - SHIFT[p], ty - SHIFT[q]),
            device_id_type=MESH,
        )

    def outgoing(n):
        return exists(-SHIFT[RING[n][0]], -SHIFT[RING[n][1]])

    def incoming(n):
        return exists(SHIFT[RING[n][0]], SHIFT[RING[n][1]])

    def send_halo(stage, own):
        buckets[stage] = dot(gather_sel[...], own).astype(BF)
        for n in range(len(RING)):

            @pl.when(outgoing(n))
            def _():
                halo_copy(stage, n).start()

    def wait_halo(stage):
        for n in range(len(RING)):

            @pl.when(incoming(n))
            def _():
                halo_copy(stage, n).wait_recv()

        again = ring.shape[1] - len(RING) * SLOT
        ring[stage, len(RING) * SLOT :, :] = ring[stage, :again, :]

    def wait_sent(stage):
        for n in range(len(RING)):

            @pl.when(outgoing(n))
            def _():
                halo_copy(stage, n).wait_send()

    def pick_own(own, into, flip):
        low = lax.broadcasted_iota(jnp.int32, (vox, lanes), 1) < chan
        step = UNROLL

        def some(i, _):
            for u in range(step):
                j = i * step + u
                first = (OFFS - 1) - 2 * j if flip else 2 * j + 1
                rows = pl.ds(pl.multiple_of(first * vox, vox), 2 * vox)
                both = dot(own_hot[rows, :], own)
                ahead, behind = both[:vox], both[vox:]
                if flip:
                    ahead, behind = behind, ahead
                at = pl.multiple_of(j * lanes, lanes)
                into[:, pl.ds(at, lanes)] = jnp.where(low, ahead, behind).astype(BF)
            return 0

        lax.fori_loop(0, (PAIRS - 2) // step, some, 0)
        last = into[:, width - chan :]
        into[:, width - chan :] = jnp.where(low, last, jnp.ones_like(last))

    def pick_halo(stage, into, flip):
        low = lax.broadcasted_iota(jnp.int32, (SLOT, lanes), 1) < chan
        for quad in range(4):
            near = ring[stage, FIRST[quad] * SLOT : (FIRST[quad] + BESIDE) * SLOT, :]
            found = dot(halo_hot[quad], near)
            for j in range(PAIRS - 2):
                k0, k1 = (OFFS - 2 * j, OFFS - 1 - 2 * j) if flip else (2 * j + 1, 2 * j + 2)
                into[quad * SLOT : (quad + 1) * SLOT, j * lanes : (j + 1) * lanes] = jnp.where(
                    low, found[k0 * SLOT : (k0 + 1) * SLOT], found[k1 * SLOT : (k1 + 1) * SLOT]
                ).astype(BF)

    def convolve(own_picked, halo_picked, weight, dims):
        edge = dot(halo_picked[...], weight[...], dims)
        high = edge.astype(BF)
        low = (edge - high.astype(F32)).astype(BF)
        inner = dot(own_picked[...], weight[...], dims)
        return inner + dot(scatter_sel[...], jnp.concatenate([high, low], axis=0))

    loads[0].wait()
    loads[1].wait()
    quads = [shell[a, b : b + 1, :][:, :SLOT] for a in range(2) for b in range(2)]
    listed = jnp.concatenate(quads, axis=1)
    by_voxel = lax.broadcasted_iota(jnp.int32, (vox, 4 * SLOT), 0) == listed
    scatter = jnp.where(by_voxel, 1.0, 0.0)
    gather = scatter.T
    gather_sel[...] = gather.astype(BF)
    scatter_sel[...] = jnp.concatenate([scatter, scatter], axis=1).astype(BF)

    both = feats[...].astype(F32)
    inputs = jnp.concatenate([both, both], axis=0).T
    pl.semaphore_wait(barrier, near_x * near_y - 1 + (tys - 1) + (tiles - 1))
    send_halo(0, inputs.astype(BF))

    loads[2].wait()
    index = nbr[...]
    outer = index - vox
    slot = jnp.bitwise_and(outer, 127)
    block = lax.shift_right_logical(outer, 7)
    position = jnp.full(index.shape, 15, jnp.int32)
    for n, (p, q) in enumerate(RING):
        position = jnp.where(block == 4 * p + q, n, position)
    position = jnp.where(jnp.logical_and(index >= vox, slot < SLOT), position, 15)
    slot = jnp.bitwise_and(slot, SLOT - 1)
    fill = jnp.zeros((32 - OFFS, vox), F32)
    stacked = [position.astype(F32), fill, slot.astype(F32), fill, index.astype(F32), fill]
    stacked = jnp.concatenate(stacked + [jnp.zeros((32, vox), F32)], axis=0).T
    table[...] = stacked

    place = lax.broadcasted_iota(jnp.int32, (4 * SLOT, vox), 0)
    quad_of = lax.shift_right_logical(place, 5)
    frame_block = 5 + 4 * lax.shift_right_logical(quad_of, 1) + jnp.bitwise_and(quad_of, 1)
    frame_row = vox + 128 * frame_block + jnp.bitwise_and(place, SLOT - 1)
    alias = jnp.where(gather > 0.5, frame_row.astype(F32), -1.0)
    alias = jnp.max(alias, axis=0, keepdims=True)
    own_hot[:vox, :] = jnp.zeros((vox, vox), BF)
    own_hot[(OFFS + 1) * vox :, :] = jnp.zeros((vox, vox), BF)
    height = 32

    def build(i, _):
        base = i * height
        entries = table[pl.ds(pl.multiple_of(base, height), height), :]
        row = lax.broadcasted_iota(jnp.int32, (height, vox), 1).astype(F32)
        for k in range(OFFS):
            entry = entries[:, 64 + k : 65 + k]
            hit = jnp.logical_or(entry == row, entry == alias)
            at = pl.multiple_of((k + 1) * vox + base, height)
            own_hot[pl.ds(at, height), :] = jnp.where(hit, 1.0, 0.0).astype(BF)
        return 0

    lax.fori_loop(0, vox // height, build, 0)

    edges = dot(gather_sel[...], stacked.astype(BF))
    position, slot = edges[:, :32], edges[:, 32:64]
    quad_of = lax.shift_right_logical(lax.broadcasted_iota(jnp.int32, position.shape, 0), 5)
    start = jnp.full(position.shape, FIRST[0], jnp.int32)
    for quad in range(1, 4):
        start = jnp.where(quad_of == quad, FIRST[quad], start)
    ahead = position - start.astype(F32)
    ahead = jnp.where(ahead < 0.0, ahead + len(RING), ahead)
    near = jnp.where(jnp.logical_and(position < 12.0, ahead < BESIDE), ahead * SLOT + slot, -1.0)
    for quad in range(4):
        halo_hot[quad, :SLOT, :] = jnp.zeros((SLOT, BESIDE * SLOT), BF)
        halo_hot[quad, (OFFS + 1) * SLOT :, :] = jnp.zeros((SLOT, BESIDE * SLOT), BF)
    row = lax.broadcasted_iota(jnp.int32, (4 * SLOT, BESIDE * SLOT), 1).astype(F32)
    for k in range(OFFS):
        hit = jnp.where(near[:, k : k + 1] == row, 1.0, 0.0).astype(BF)
        for quad in range(4):
            halo_hot[quad, (k + 1) * SLOT : (k + 2) * SLOT, :] = hit[
                quad * SLOT : (quad + 1) * SLOT
            ]

    def forward_weight(weight, forward):
        for k in range(OFFS):
            value = weight[k]
            forward[k * chan : (k + 1) * chan, :] = jnp.concatenate([value, value], axis=1)
        forward[width:, :] = jnp.zeros((chan, lanes), BF)

    def turned_weight(weight, turned):
        for j in range(PAIRS - 2):
            left = weight[2 * j]
            right = weight[2 * j + 1] if 2 * j + 1 < OFFS else jnp.zeros((chan, chan), BF)
            beside = jnp.concatenate([left, right], axis=1)
            turned[:chan, lanes * j : lanes * (j + 1)] = beside
            turned[chan:, lanes * j : lanes * (j + 1)] = beside

    def twice(bias):
        return jnp.concatenate([bias[...], bias[...]], axis=1)

    def ty_copy(g, d, c):
        to = lax.rem(ty + d, tys)
        at = pl.multiple_of(to * quarter + c * chunk, chunk)
        return pltpu.make_async_remote_copy(
            src_ref=part.at[g, pl.ds(at, chunk)],
            dst_ref=rs1.at[g, d, pl.ds(pl.multiple_of(c * chunk, chunk), chunk)],
            send_sem=s1.at[g, d, c],
            recv_sem=r1.at[g, d, c],
            device_id=device(tx, to),
            device_id_type=MESH,
        )

    def tile_copy(g, d):
        to = lax.rem(tx + d, tiles)
        at = pl.multiple_of(lax.rem(to, owners) * chunk, chunk)
        return pltpu.make_async_remote_copy(
            src_ref=mid.at[g, pl.ds(at, chunk)],
            dst_ref=rs2.at[g, d],
            send_sem=s2.at[g, d],
            recv_sem=r2.at[g, d],
            device_id=device(to, ty),
            device_id_type=MESH,
        )

    def chunk_rows(y, c):
        return pl.ds(pl.multiple_of(y * quarter + lax.rem(c, owners) * chunk, chunk), chunk)

    def back_tile(g, d, c):
        return pltpu.make_async_remote_copy(
            src_ref=full.at[g, chunk_rows(ty, c)],
            dst_ref=full.at[g, chunk_rows(ty, c)],
            send_sem=s3.at[g, d],
            recv_sem=r3.at[g, d],
            device_id=device(lax.rem(tx + d, tiles), ty),
            device_id_type=MESH,
        )

    def back_ty(g, d, y, c):
        at = lax.rem(c, owners)
        return pltpu.make_async_remote_copy(
            src_ref=full.at[g, chunk_rows(y, c)],
            dst_ref=full.at[g, chunk_rows(y, c)],
            send_sem=s4.at[g, d, at],
            recv_sem=r4.at[g, d, at],
            device_id=device(tx, lax.rem(ty + d, tys)),
            device_id_type=MESH,
        )

    def owned(x, body):
        if owners >= tiles:
            body()
        else:
            pl.when(x < owners)(body)

    def reduce_start(g, gradient, edge, own_picked, halo_picked):
        turned = gradient.astype(F32).T[:chan].astype(BF)
        edge_turned = edge.astype(F32).T[:chan].astype(BF)
        terms = dot(turned, own_picked[...]) + dot(edge_turned, halo_picked[...])
        for j in range(PAIRS - 2):
            part[g, j * chan : (j + 1) * chan, :] = terms[
                :, lanes * j : lanes * (j + 1)
            ].astype(BF)
        part[g, (PAIRS - 2) * chan :, :] = jnp.zeros((2 * chan, lanes), BF)
        for i in range(owners):
            for d in range(1, tys):
                ty_copy(g, d, lax.rem(tx + 1 + i, owners)).start()

    def reduce_tiles(g):
        for d in [*range(1, tiles), 0]:
            c = lax.rem(tx + d, tiles)

            def body():
                for e in range(1, tys):
                    ty_copy(g, e, lax.rem(c, owners)).wait_recv()
                total = part[g, chunk_rows(ty, c), :].astype(F32)
                rows = pl.ds(pl.multiple_of(lax.rem(c, owners) * chunk, chunk), chunk)
                for e in range(1, tys):
                    total = total + rs1[g, e, rows, :].astype(F32)
                turned = []
                for j in range(chunk // chan):
                    flat = total[j * chan : (j + 1) * chan].T
                    turned.append(jnp.concatenate([flat[:chan], flat[chan:]], axis=1))
                mid[g, rows, :] = jnp.concatenate(turned, axis=0).astype(BF)
                if d:
                    tile_copy(g, d).start()

            owned(c, body)

    def spread_tiles(g):
        def body():
            for d in range(1, tiles):
                tile_copy(g, d).wait_recv()
            at = pl.multiple_of(lax.rem(tx, owners) * chunk, chunk)
            total = mid[g, pl.ds(at, chunk), :].astype(F32)
            for d in range(1, tiles):
                total = total + rs2[g, d].astype(F32)
            full[g, chunk_rows(ty, tx), :] = total.astype(BF)
            for d in range(1, tiles):
                back_tile(g, d, tx).start()
            for d in range(1, tys):
                back_ty(g, d, ty, tx).start()

        owned(tx, body)

    def spread_ty(g):
        for d in range(1, tiles):
            source = lax.rem(tx - d + tiles, tiles)

            def body():
                back_tile(g, d, source).wait_recv()
                for e in range(1, tys):
                    back_ty(g, e, ty, source).start()

            owned(source, body)

    def finish(g):
        for d in range(1, tys):
            for c in range(owners):
                back_ty(g, d, lax.rem(ty - d + tys, tys), jnp.int32(c)).wait_recv()
        full_out[g] = full[g]

    def drain(g):
        for d in range(1, tys):
            for c in range(owners):
                ty_copy(g, d, c).wait_send()
                back_ty(g, d, ty, jnp.int32(c)).wait_send()
        for d in range(1, tiles):
            owned(lax.rem(tx + d, tiles), lambda: tile_copy(g, d).wait_send())
            owned(tx, lambda: back_tile(g, d, tx).wait_send())

    plain = ((1,), (0,))
    across = ((1,), (1,))
    pick_own(inputs.astype(BF), own_a, False)
    loads[3].wait()
    forward_weight(w1, wf1)
    wait_halo(0)
    pick_halo(0, halo_a, False)
    first = convolve(own_a, halo_a, wf1, plain) + twice(b1)
    hidden = (first * jax.nn.sigmoid(first)).astype(BF)
    send_halo(1, hidden)
    pick_own(hidden, own_b, False)
    loads[4].wait()
    loads[5].wait()
    forward_weight(w2, wf2)
    upstream = cot[...].astype(F32)
    upstream = jnp.concatenate([upstream, upstream], axis=0).T
    wait_halo(1)
    pick_halo(1, halo_b, False)
    second = convolve(own_b, halo_b, wf2, plain) + twice(b2)
    grad_out = (upstream * silu_slope(inputs + second)).astype(BF)

    send_halo(2, grad_out)
    reduce_start(1, grad_out, buckets[2], own_b, halo_b)
    pick_own(grad_out, own_c, True)
    turned_weight(w2, wt2)
    wait_halo(2)
    pick_halo(2, halo_c, True)
    back = convolve(own_c, halo_c, wt2, across)
    grad_pre = (back * silu_slope(first)).astype(BF)
    send_halo(3, grad_pre)
    reduce_start(0, grad_pre, buckets[3], own_a, halo_a)
    reduce_tiles(1)
    pick_own(grad_pre, own_c, True)
    turned_weight(w1, wt1)
    spread_tiles(1)
    wait_halo(3)
    pick_halo(3, halo_c, True)
    back = convolve(own_c, halo_c, wt1, across)
    gf_out[...] = (grad_out.astype(F32) + back).T[:chan]
    reduce_tiles(0)
    spread_ty(1)
    spread_tiles(0)
    spread_ty(0)
    finish(1)
    finish(0)
    for stage in range(4):
        wait_sent(stage)
    drain(1)
    drain(0)


def unpack(scale, gf, full, gf_out, gw1_out, gb1_out, gw2_out, gb2_out):
    gf_out[0, 0] = gf[...]
    chan = gf.shape[0]
    for g, gw_out, gb_out in ((0, gw1_out, gb1_out), (1, gw2_out, gb2_out)):
        for j in range(PAIRS - 2):
            value = full[g, j * chan : (j + 1) * chan, :].astype(F32) * scale
            gw_out[2 * j] = value[:, :chan]
            if 2 * j + 1 < OFFS:
                gw_out[2 * j + 1] = value[:, chan:]
            else:
                gb_out[...] = value[:1, chan:]


def per_device(feats, weight1, bias1, weight2, bias2, cotangent, neighbors, shell):
    tiles, chs, subs = (lax.axis_size(a) for a in ("tile", "ch", "sub"))
    chan, vox = feats.shape[2:]
    tys = chs * subs
    scale = 1.0 / math.sqrt(vox * tiles * tys)
    rows = PAIRS * chan
    quarter = rows // tys
    chunk = max(chan, quarter // tiles)
    owners = quarter // chunk
    wide = (PAIRS - 2) * 2 * chan
    lanes = 2 * chan
    edge = 4 * SLOT
    vmem = pl.BlockSpec(memory_space=pltpu.VMEM)
    hbm = pl.BlockSpec(memory_space=pl.ANY)
    dma = pltpu.SemaphoreType.DMA
    gf, full = pl.pallas_call(
        functools.partial(kernel, tiles, chs, subs),
        out_shape=(
            jax.ShapeDtypeStruct((chan, vox), F32),
            jax.ShapeDtypeStruct((2, rows, lanes), BF),
        ),
        in_specs=[hbm, hbm, vmem, hbm, vmem, hbm, hbm, hbm],
        out_specs=(vmem, vmem),
        scratch_shapes=[
            pltpu.VMEM((chan, vox), BF),
            pltpu.VMEM(weight1.shape, BF),
            pltpu.VMEM(weight2.shape, BF),
            pltpu.VMEM((chan, vox), BF),
            pltpu.VMEM((OFFS, vox), jnp.int32),
            pltpu.VMEM(shell.shape[2:], jnp.int32),
            dma((6,)),
            pltpu.VMEM(((OFFS + 2) * vox, vox), BF),
            pltpu.VMEM((4, (OFFS + 2) * SLOT, BESIDE * SLOT), BF),
            pltpu.VMEM((4, (len(RING) + 3) * SLOT, lanes), BF),
            pltpu.VMEM((vox, wide), BF),
            pltpu.VMEM((vox, wide), BF),
            pltpu.VMEM((vox, wide), BF),
            pltpu.VMEM((edge, wide), BF),
            pltpu.VMEM((edge, wide), BF),
            pltpu.VMEM((edge, wide), BF),
            pltpu.VMEM((wide, lanes), BF),
            pltpu.VMEM((wide, lanes), BF),
            pltpu.VMEM((lanes, wide), BF),
            pltpu.VMEM((lanes, wide), BF),
            pltpu.VMEM((edge, vox), BF),
            pltpu.VMEM((vox, 2 * edge), BF),
            pltpu.VMEM((4, edge, lanes), BF),
            pltpu.VMEM((vox, 128), F32),
            pltpu.VMEM((2, rows, lanes), BF),
            pltpu.VMEM((2, tys, quarter, lanes), BF),
            pltpu.VMEM((2, quarter, lanes), BF),
            pltpu.VMEM((2, tiles, chunk, lanes), BF),
            pltpu.VMEM((2, rows, lanes), BF),
            dma((4, len(RING))),
            dma((4, len(RING))),
            dma((2, tys, owners)),
            dma((2, tys, owners)),
            dma((2, tiles)),
            dma((2, tiles)),
            dma((2, tiles)),
            dma((2, tiles)),
            dma((2, tys, owners)),
            dma((2, tys, owners)),
        ],
        compiler_params=pltpu.CompilerParams(
            collective_id=0, has_side_effects=True, vmem_limit_bytes=48 * 1024 * 1024
        ),
    )(feats, weight1, bias1[None], weight2, bias2[None], cotangent, neighbors, shell)
    gf, gw1, gb1, gw2, gb2 = pl.pallas_call(
        functools.partial(unpack, scale),
        out_shape=(
            jax.ShapeDtypeStruct((1, 1, chan, vox), F32),
            jax.ShapeDtypeStruct((OFFS, chan, chan), F32),
            jax.ShapeDtypeStruct((1, chan), F32),
            jax.ShapeDtypeStruct((OFFS, chan, chan), F32),
            jax.ShapeDtypeStruct((1, chan), F32),
        ),
        in_specs=[vmem] * 2,
        out_specs=(vmem,) * 5,
        compiler_params=pltpu.CompilerParams(vmem_limit_bytes=16 * 1024 * 1024),
    )(gf, full)
    return gf, gw1, gb1[0], gw2, gb2[0]


def solution(mesh):
    placed = (
        P(("parts", "tile"), ("ch", "sub"), None, None),
        P(),
        P(),
        P(),
        P(),
        P(("parts", "tile"), ("ch", "sub"), None, None),
        P(("parts", "tile"), ("ch", "sub"), None, None),
        P(("parts", "tile"), ("ch", "sub"), None, None, None),
    )
    return jax.shard_map(
        per_device,
        mesh=mesh,
        in_specs=placed,
        out_specs=(
            P(("parts", "tile"), ("ch", "sub"), None, None),
            P("parts", None, None),
            P("parts"),
            P("parts", None, None),
            P("parts"),
        ),
        check_vma=False,
    )
```

time: 59.9 us -> 47.1 us (0.79)
  Pallas kernels: 52 us -> 42.5 us
  local copies, waits for them, and re-layouts: 6.92 us -> 3.57 us
    pallas_call x1 -> x2, Pallas kernels: 52 us -> 42.5 us  [the longest x1 41.1 us: per_device(): pl.pallas_call(functools.partial(kernel, tiles, chs, subs), out_shape=(ja...]
    unnamed x20 -> x15, local copies, waits for them, and re-layouts: 6.92 us -> 3.57 us
where the time goes in v2:
time: 47.1 us; the launch traced here: 46.8 us
  Pallas kernels  42.5 us (90%)
  local copies, waits for them, and re-layouts  3.57 us (8%)
  between operations  0.7 us (1%)
    pallas_call x1, Pallas kernels, per_device(): pl.pallas_call(functools.partial(kernel, tiles, chs, subs), out_shape=(ja...  41.1 us
    unnamed x15, local copies, waits for them, and re-layouts  3.57 us
    pallas_call x1, Pallas kernels, per_device(): pl.pallas_call(functools.partial(unpack, scale), out_shape=(jax.ShapeDtyp...  1.45 us

profile of v2, /device:TPU:0, one launch (start us, length us, event | category | flops | bytes accessed | tf_op | source)
XLA Modules:
  0.0 46.8 jit_solution(5383858840895340893)
XLA Ops:
  0.6 0.0 copy-start.2
  0.6 0.0 copy-start.4
  0.7 0.0 copy-start.5
  0.7 0.0 copy-start.6
  0.7 0.8 %copy.13.nbr_in = s32[1,1,27,256]{3,2,1,0:T(8,128)S(1)} copy(s32[1,1,27,256]{3,1,2,0:T(1,128)} %param.14) | data formatting | bytes 55296 | tf_op args[6]
  1.4 0.0 copy-done.2
  1.4 0.0 copy-done.4
  1.4 0.0 copy-done.5
  1.5 0.0 copy-done.6
  1.5 0.0 copy-start
  1.5 1.0 %copy-done = bf16[27,64,64]{2,1,0:T(8,128)(2,1)S(1)} copy-done((bf16[27,64,64]{2,1,0:T(8,128)(2,1)S(1)}, bf16[27,64,64]{2,1,0:T(8,128)(2,1)}, u32[]{:S(2)}) %copy-start) | copy-done | bytes 221208
  2.5 0.0 copy-start.1
  2.5 1.0 %copy-done.1 = bf16[27,64,64]{2,1,0:T(8,128)(2,1)S(1)} copy-done((bf16[27,64,64]{2,1,0:T(8,128)(2,1)S(1)}, bf16[27,64,64]{2,1,0:T(8,128)(2,1)}, u32[]{:S(2)}) %copy-start.1) | copy-done | bytes 221208
  3.5 0.0 copy-start.3
  3.5 0.8 %copy-done.3 = bf16[1,1,64,256]{3,2,1,0:T(8,128)(2,1)S(1)} copy-done((bf16[1,1,64,256]{3,2,1,0:T(8,128)(2,1)S(1)}, bf16[1,1,64,256]{3,2,1,0:T(8,128)(2,1)}, u32[]{:S(2)}) %copy-start.3) | copy-done | bytes 32792
  4.3 41.1 %shard_map.119 = (f32[64,256]{1,0:T(8,128)S(1)}, bf16[2,1024,128]{2,1,0:T(8,128)(2,1)S(1)}) custom-call(bf16[1,1,64,256]{3,2,1,0:T(8,128)(2,1)S(1)} %copy-done.2, bf16[27,64,64]{2,1,0:T(8,128)(2,1)S(1)} %copy-done, f32[1,64]{1,0:T(1,128)S(1)} %bitcast.4, bf16[27,64,64]{2,1,0:T(8,128)(2,1)S(1)} %copy-done.1, f32[1,64]{1,0:T(1,128)S(1)} %bitcast.5, ...), custom_call_target="tpu_custom_call" | custom-call | tf_op jit(solution)/shard_map/pallas_call | solution.py:489
  45.3 1.5 %shard_map.120 = (f32[1,1,64,256]{3,2,1,0:T(8,128)}, f32[27,64,64]{2,1,0:T(8,128)}, f32[1,64]{1,0:T(1,128)}, f32[27,64,64]{2,1,0:T(8,128)}, f32[1,64]{1,0:T(1,128)}) custom-call(f32[64,256]{1,0:T(8,128)S(1)} %get-tuple-element.12.gf, bf16[2,1024,128]{2,1,0:T(8,128)(2,1)S(1)} %get-tuple-element.13.full), custom_call_target="tpu_custom_call" | custom-call | tf_op jit(solution)/shard_map/pallas_call | solution.py:542
Async XLA Ops:
  0.6 0.8 %copy-start.2 = (bf16[1,1,64,256]{3,2,1,0:T(8,128)(2,1)S(1)}, bf16[1,1,64,256]{3,2,1,0:T(8,128)(2,1)}, u32[]{:S(2)}) copy-start(bf16[1,1,64,256]{3,2,1,0:T(8,128)(2,1)} %feats_in.1) | copy-start | bytes 98308
  0.6 0.8 %copy-start.4 = (s32[1,1,2,2,128]{4,3,2,1,0:T(2,128)S(1)}, s32[1,1,2,2,128]{4,3,2,1,0:T(2,128)}, u32[]{:S(2)}) copy-start(s32[1,1,2,2,128]{4,3,2,1,0:T(2,128)} %shell_in.1) | copy-start | bytes 6148
  0.7 0.8 %copy-start.5 = (f32[64]{0:T(128)S(1)}, f32[64]{0:T(128)}, u32[]{:S(2)}) copy-start(f32[64]{0:T(128)} %param.10) | copy-start | bytes 772
  0.7 0.8 %copy-start.6 = (f32[64]{0:T(128)S(1)}, f32[64]{0:T(128)}, u32[]{:S(2)}) copy-start(f32[64]{0:T(128)} %param.12) | copy-start | bytes 772
  1.5 1.0 %copy-start = (bf16[27,64,64]{2,1,0:T(8,128)(2,1)S(1)}, bf16[27,64,64]{2,1,0:T(8,128)(2,1)}, u32[]{:S(2)}) copy-start(bf16[27,64,64]{2,1,0:T(8,128)(2,1)} %w1_in.1) | copy-start | bytes 663556
  2.5 1.0 %copy-start.1 = (bf16[27,64,64]{2,1,0:T(8,128)(2,1)S(1)}, bf16[27,64,64]{2,1,0:T(8,128)(2,1)}, u32[]{:S(2)}) copy-start(bf16[27,64,64]{2,1,0:T(8,128)(2,1)} %w2_in.1) | copy-start | bytes 663556
  3.5 0.8 %copy-start.3 = (bf16[1,1,64,256]{3,2,1,0:T(8,128)(2,1)S(1)}, bf16[1,1,64,256]{3,2,1,0:T(8,128)(2,1)}, u32[]{:S(2)}) copy-start(bf16[1,1,64,256]{3,2,1,0:T(8,128)(2,1)} %cot_in.1) | copy-start | bytes 98308

commit v3 on v2

--- a/solution.py
+++ b/solution.py
@@ -14,7 +14,7 @@
 SLOT = 32
 PAIRS = 16
 OFFS = 27
-UNROLL = 7
+UNROLL = 14
 RING = [
     (0, 0), (0, 1), (0, 2), (0, 3), (1, 3), (2, 3),
     (3, 3), (3, 2), (3, 1), (3, 0), (2, 0), (1, 0),
@@ -36,9 +36,9 @@
 
 def kernel(
     tiles, chs, subs,
-    feats_in, w1_in, b1, w2_in, b2, cot_in, nbr_in, shell_in,
+    feats_in, w1_in, b1_in, w2_in, b2_in, cot_in, nbr_in, shell_in,
     gf_out, full_out,
-    feats, w1, w2, cot, nbr, shell, in_sem,
+    feats, w1, b1, w2, b2, cot, nbr, shell, in_sem,
     own_hot, halo_hot, ring, own_a, own_b, own_c, halo_a, halo_b, halo_c,
     wf1, wf2, wt1, wt2, gather_sel, scatter_sel, buckets, table,
     part, rs1, mid, rs2, full,
@@ -60,10 +60,12 @@
         for i, (src, dst) in enumerate((
             (feats_in.at[0, 0], feats),
             (shell_in.at[0, 0], shell),
-            (nbr_in.at[0, 0], nbr),
+            (nbr_in.at[:, 0], nbr),
             (w1_in, w1),
             (cot_in.at[0, 0], cot),
             (w2_in, w2),
+            (b1_in, b1),
+            (b2_in, b2),
         ))
     ]
     for load in loads:
@@ -398,13 +400,18 @@
                 back_ty(g, d, lax.rem(ty - d + tys, tys), jnp.int32(c)).wait_recv()
         full_out[g] = full[g]
 
-    def drain(g):
+    def drain_sums(g):
         for d in range(1, tys):
             for c in range(owners):
                 ty_copy(g, d, c).wait_send()
+        for d in range(1, tiles):
+            owned(lax.rem(tx + d, tiles), lambda: tile_copy(g, d).wait_send())
+
+    def drain_back(g):
+        for d in range(1, tys):
+            for c in range(owners):
                 back_ty(g, d, ty, jnp.int32(c)).wait_send()
         for d in range(1, tiles):
-            owned(lax.rem(tx + d, tiles), lambda: tile_copy(g, d).wait_send())
             owned(tx, lambda: back_tile(g, d, tx).wait_send())
 
     plain = ((1,), (0,))
@@ -412,6 +419,8 @@
     pick_own(inputs.astype(BF), own_a, False)
     loads[3].wait()
     forward_weight(w1, wf1)
+    loads[6].wait()
+    loads[7].wait()
     wait_halo(0)
     pick_halo(0, halo_a, False)
     first = convolve(own_a, halo_a, wf1, plain) + twice(b1)
@@ -421,6 +430,7 @@
     loads[4].wait()
     loads[5].wait()
     forward_weight(w2, wf2)
+    turned_weight(w2, wt2)
     upstream = cot[...].astype(F32)
     upstream = jnp.concatenate([upstream, upstream], axis=0).T
     wait_halo(1)
@@ -431,7 +441,7 @@
     send_halo(2, grad_out)
     reduce_start(1, grad_out, buckets[2], own_b, halo_b)
     pick_own(grad_out, own_c, True)
-    turned_weight(w2, wt2)
+    turned_weight(w1, wt1)
     wait_halo(2)
     pick_halo(2, halo_c, True)
     back = convolve(own_c, halo_c, wt2, across)
@@ -440,22 +450,23 @@
     reduce_start(0, grad_pre, buckets[3], own_a, halo_a)
     reduce_tiles(1)
     pick_own(grad_pre, own_c, True)
-    turned_weight(w1, wt1)
     spread_tiles(1)
     wait_halo(3)
     pick_halo(3, halo_c, True)
+    reduce_tiles(0)
+    spread_ty(1)
     back = convolve(own_c, halo_c, wt1, across)
     gf_out[...] = (grad_out.astype(F32) + back).T[:chan]
-    reduce_tiles(0)
-    spread_ty(1)
     spread_tiles(0)
-    spread_ty(0)
-    finish(1)
-    finish(0)
     for stage in range(4):
         wait_sent(stage)
-    drain(1)
-    drain(0)
+    drain_sums(1)
+    spread_ty(0)
+    drain_sums(0)
+    finish(1)
+    drain_back(1)
+    finish(0)
+    drain_back(0)
 
 
 def unpack(scale, gf, full, gf_out, gw1_out, gb1_out, gw2_out, gb2_out):
@@ -484,7 +495,7 @@
     lanes = 2 * chan
     edge = 4 * SLOT
     vmem = pl.BlockSpec(memory_space=pltpu.VMEM)
-    hbm = pl.BlockSpec(memory_space=pl.ANY)
+    hbm = pl.BlockSpec(memory_space=pltpu.HBM)
     dma = pltpu.SemaphoreType.DMA
     gf, full = pl.pallas_call(
         functools.partial(kernel, tiles, chs, subs),
@@ -492,16 +503,18 @@
             jax.ShapeDtypeStruct((chan, vox), F32),
             jax.ShapeDtypeStruct((2, rows, lanes), BF),
         ),
-        in_specs=[hbm, hbm, vmem, hbm, vmem, hbm, hbm, hbm],
+        in_specs=[hbm] * 8,
         out_specs=(vmem, vmem),
         scratch_shapes=[
             pltpu.VMEM((chan, vox), BF),
             pltpu.VMEM(weight1.shape, BF),
+            pltpu.VMEM((1, chan), F32),
             pltpu.VMEM(weight2.shape, BF),
+            pltpu.VMEM((1, chan), F32),
             pltpu.VMEM((chan, vox), BF),
             pltpu.VMEM((OFFS, vox), jnp.int32),
             pltpu.VMEM(shell.shape[2:], jnp.int32),
-            dma((6,)),
+            dma((8,)),
             pltpu.VMEM(((OFFS + 2) * vox, vox), BF),
             pltpu.VMEM((4, (OFFS + 2) * SLOT, BESIDE * SLOT), BF),
             pltpu.VMEM((4, (len(RING) + 3) * SLOT, lanes), BF),
@@ -536,9 +549,9 @@
             dma((2, tys, owners)),
         ],
         compiler_params=pltpu.CompilerParams(
-            collective_id=0, has_side_effects=True, vmem_limit_bytes=48 * 1024 * 1024
+            collective_id=0, has_side_effects=True, vmem_limit_bytes=63 * 1024 * 1024
         ),
-    )(feats, weight1, bias1[None], weight2, bias2[None], cotangent, neighbors, shell)
+    )(feats, weight1, bias1[None], weight2, bias2[None], cotangent, neighbors.reshape(OFFS, 1, vox), shell)
     gf, gw1, gb1, gw2, gb2 = pl.pallas_call(
         functools.partial(unpack, scale),
         out_shape=(

time: 47.1 us -> 43.7 us (0.928)
  local copies, waits for them, and re-layouts: 3.57 us -> 1.87 us
  Pallas kernels: 42.5 us -> 41 us
    unnamed x15 -> x4, local copies, waits for them, and re-layouts: 3.57 us -> 1.87 us
    pallas_call x1, Pallas kernels: 41.1 us -> 39.5 us  [per_device(): pl.pallas_call(functools.partial(kernel, tiles, chs, subs), out_shape=(ja...]
where the time goes in v3:
time: 43.7 us; the launch traced here: 43.5 us
  Pallas kernels  41 us (94%)
  local copies, waits for them, and re-layouts  1.87 us (4%)
  between operations  0.65 us (1%)
    pallas_call x1, Pallas kernels, per_device(): pl.pallas_call(functools.partial(kernel, tiles, chs, subs), out_shape=(ja...  39.5 us
    unnamed x4, local copies, waits for them, and re-layouts  1.87 us
    pallas_call x1, Pallas kernels, per_device(): pl.pallas_call(functools.partial(unpack, scale), out_shape=(jax.ShapeDtyp...  1.45 us

profile of v3, /device:TPU:0, one launch (start us, length us, event | category | flops | bytes accessed | tf_op | source)
XLA Modules:
  0.0 43.5 jit_solution(9117627202220034712)
XLA Ops:
  0.6 39.5 %shard_map.119 = (f32[64,256]{1,0:T(8,128)}, bf16[2,1024,128]{2,1,0:T(8,128)(2,1)}) custom-call(bf16[1,1,64,256]{3,2,1,0:T(8,128)(2,1)} %feats_in.1, bf16[27,64,64]{2,1,0:T(8,128)(2,1)} %w1_in.1, f32[1,64]{1,0:T(1,128)} %bitcast.6, bf16[27,64,64]{2,1,0:T(8,128)(2,1)} %w2_in.1, f32[1,64]{1,0:T(1,128)} %bitcast.7, bf16[1,1,64,256]{3,2,1,0:T(8,128)(2,1)} %cot_in.1, ...), custom_call_target="tpu_custom_call" | custom-call | tf_op jit(solution)/shard_map/pallas_call | solution.py:500
  40.2 0.0 copy-start
  40.2 1.0 %copy-done = bf16[2,1024,128]{2,1,0:T(8,128)(2,1)S(1)} copy-done((bf16[2,1024,128]{2,1,0:T(8,128)(2,1)S(1)}, bf16[2,1024,128]{2,1,0:T(8,128)(2,1)}, u32[]{:S(2)}) %copy-start) | copy-done | bytes 524312
  41.2 0.0 copy-start.1
  41.2 0.8 %copy-done.1 = f32[64,256]{1,0:T(8,128)S(1)} copy-done((f32[64,256]{1,0:T(8,128)S(1)}, f32[64,256]{1,0:T(8,128)}, u32[]{:S(2)}) %copy-start.1) | copy-done | bytes 65560
  42.1 1.4 %shard_map.120 = (f32[1,1,64,256]{3,2,1,0:T(8,128)}, f32[27,64,64]{2,1,0:T(8,128)}, f32[1,64]{1,0:T(1,128)}, f32[27,64,64]{2,1,0:T(8,128)}, f32[1,64]{1,0:T(1,128)}) custom-call(f32[64,256]{1,0:T(8,128)S(1)} %copy-done.1, bf16[2,1024,128]{2,1,0:T(8,128)(2,1)S(1)} %copy-done), custom_call_target="tpu_custom_call" | custom-call | tf_op jit(solution)/shard_map/pallas_call | solution.py:555
Async XLA Ops:
  40.2 1.0 %copy-start = (bf16[2,1024,128]{2,1,0:T(8,128)(2,1)S(1)}, bf16[2,1024,128]{2,1,0:T(8,128)(2,1)}, u32[]{:S(2)}) copy-start(bf16[2,1024,128]{2,1,0:T(8,128)(2,1)} %get-tuple-element.13.full) | copy-start | bytes 1572868
  41.2 0.8 %copy-start.1 = (f32[64,256]{1,0:T(8,128)S(1)}, f32[64,256]{1,0:T(8,128)}, u32[]{:S(2)}) copy-start(f32[64,256]{1,0:T(8,128)} %get-tuple-element.12.gf) | copy-start | bytes 196612

commit v4 on v3

--- a/solution.py
+++ b/solution.py
@@ -38,7 +38,7 @@
     tiles, chs, subs,
     feats_in, w1_in, b1_in, w2_in, b2_in, cot_in, nbr_in, shell_in,
     gf_out, full_out,
-    feats, w1, b1, w2, b2, cot, nbr, shell, in_sem,
+    feats, w1, b1, w2, b2, cot, nbr, shell, in_sem, gf, out_sem,
     own_hot, halo_hot, ring, own_a, own_b, own_c, halo_a, halo_b, halo_c,
     wf1, wf2, wt1, wt2, gather_sel, scatter_sel, buckets, table,
     part, rs1, mid, rs2, full,
@@ -70,6 +70,14 @@
     ]
     for load in loads:
         load.start()
+    stores = [
+        pltpu.make_async_copy(src, dst, out_sem.at[i])
+        for i, (src, dst) in enumerate((
+            (full.at[0], full_out.at[0]),
+            (full.at[1], full_out.at[1]),
+            (gf, gf_out),
+        ))
+    ]
 
     def device(x, y):
         return {"tile": x, "ch": y // subs, "sub": y % subs}
@@ -398,7 +406,7 @@
         for d in range(1, tys):
             for c in range(owners):
                 back_ty(g, d, lax.rem(ty - d + tys, tys), jnp.int32(c)).wait_recv()
-        full_out[g] = full[g]
+        stores[g].start()
 
     def drain_sums(g):
         for d in range(1, tys):
@@ -456,7 +464,8 @@
     reduce_tiles(0)
     spread_ty(1)
     back = convolve(own_c, halo_c, wt1, across)
-    gf_out[...] = (grad_out.astype(F32) + back).T[:chan]
+    gf[...] = (grad_out.astype(F32) + back).T[:chan]
+    stores[2].start()
     spread_tiles(0)
     for stage in range(4):
         wait_sent(stage)
@@ -467,19 +476,42 @@
     drain_back(1)
     finish(0)
     drain_back(0)
-
-
-def unpack(scale, gf, full, gf_out, gw1_out, gb1_out, gw2_out, gb2_out):
-    gf_out[0, 0] = gf[...]
+    for store in stores:
+        store.wait()
+
+
+def unpack(
+    scale, gf_in, full_in, gf_out, gw1_out, gb1_out, gw2_out, gb2_out,
+    gf, full, gw, gb1, gb2, in_sem, out_sem,
+):
     chan = gf.shape[0]
-    for g, gw_out, gb_out in ((0, gw1_out, gb1_out), (1, gw2_out, gb2_out)):
+    loads = [
+        pltpu.make_async_copy(full_in.at[g], full.at[g], in_sem.at[g]) for g in range(2)
+    ] + [pltpu.make_async_copy(gf_in, gf, in_sem.at[2])]
+    for load in loads:
+        load.start()
+    stores = []
+
+    def store(src, dst):
+        copy = pltpu.make_async_copy(src, dst, out_sem.at[len(stores)])
+        copy.start()
+        stores.append(copy)
+
+    for g, gw_out, gb, gb_out in ((0, gw1_out, gb1, gb1_out), (1, gw2_out, gb2, gb2_out)):
+        loads[g].wait()
         for j in range(PAIRS - 2):
             value = full[g, j * chan : (j + 1) * chan, :].astype(F32) * scale
-            gw_out[2 * j] = value[:, :chan]
+            gw[g, 2 * j] = value[:, :chan]
             if 2 * j + 1 < OFFS:
-                gw_out[2 * j + 1] = value[:, chan:]
+                gw[g, 2 * j + 1] = value[:, chan:]
             else:
-                gb_out[...] = value[:1, chan:]
+                gb[...] = value[:1, chan:]
+        store(gw.at[g], gw_out)
+        store(gb, gb_out)
+    loads[2].wait()
+    store(gf, gf_out.at[0, 0])
+    for copy in stores:
+        copy.wait()
 
 
 def per_device(feats, weight1, bias1, weight2, bias2, cotangent, neighbors, shell):
@@ -494,7 +526,6 @@
     wide = (PAIRS - 2) * 2 * chan
     lanes = 2 * chan
     edge = 4 * SLOT
-    vmem = pl.BlockSpec(memory_space=pltpu.VMEM)
     hbm = pl.BlockSpec(memory_space=pltpu.HBM)
     dma = pltpu.SemaphoreType.DMA
     gf, full = pl.pallas_call(
@@ -504,7 +535,7 @@
             jax.ShapeDtypeStruct((2, rows, lanes), BF),
         ),
         in_specs=[hbm] * 8,
-        out_specs=(vmem, vmem),
+        out_specs=(hbm, hbm),
         scratch_shapes=[
             pltpu.VMEM((chan, vox), BF),
             pltpu.VMEM(weight1.shape, BF),
@@ -515,6 +546,8 @@
             pltpu.VMEM((OFFS, vox), jnp.int32),
             pltpu.VMEM(shell.shape[2:], jnp.int32),
             dma((8,)),
+            pltpu.VMEM((chan, vox), F32),
+            dma((3,)),
             pltpu.VMEM(((OFFS + 2) * vox, vox), BF),
             pltpu.VMEM((4, (OFFS + 2) * SLOT, BESIDE * SLOT), BF),
             pltpu.VMEM((4, (len(RING) + 3) * SLOT, lanes), BF),
@@ -561,9 +594,18 @@
             jax.ShapeDtypeStruct((OFFS, chan, chan), F32),
             jax.ShapeDtypeStruct((1, chan), F32),
         ),
-        in_specs=[vmem] * 2,
-        out_specs=(vmem,) * 5,
-        compiler_params=pltpu.CompilerParams(vmem_limit_bytes=16 * 1024 * 1024),
+        in_specs=[hbm] * 2,
+        out_specs=(hbm,) * 5,
+        scratch_shapes=[
+            pltpu.VMEM((chan, vox), F32),
+            pltpu.VMEM((2, rows, lanes), BF),
+            pltpu.VMEM((2, OFFS, chan, chan), F32),
+            pltpu.VMEM((1, chan), F32),
+            pltpu.VMEM((1, chan), F32),
+            dma((3,)),
+            dma((5,)),
+        ],
+        compiler_params=pltpu.CompilerParams(vmem_limit_bytes=63 * 1024 * 1024),
     )(gf, full)
     return gf, gw1, gb1[0], gw2, gb2[0]
 

time: 43.7 us -> 42.6 us (0.975)
  local copies, waits for them, and re-layouts: 1.87 us -> 0 us
  Pallas kernels: 41 us -> 41.8 us
    unnamed x4 -> x0, local copies, waits for them, and re-layouts: 1.87 us -> none
    pallas_call x1, Pallas kernels: 1.45 us -> 2.42 us  [per_device(): pl.pallas_call(functools.partial(unpack, scale), out_shape=(jax.ShapeDtyp...]
where the time goes in v4:
time: 42.6 us; the launch traced here: 42.4 us
  Pallas kernels  41.8 us (98%)
  between operations  0.64 us (2%)
    pallas_call x1, Pallas kernels, per_device(): pl.pallas_call(functools.partial(kernel, tiles, chs, subs), out_shape=(ja...  39.4 us
    pallas_call x1, Pallas kernels, per_device(): pl.pallas_call(functools.partial(unpack, scale), out_shape=(jax.ShapeDtyp...  2.42 us

profile of v4, /device:TPU:0, one launch (start us, length us, event | category | flops | bytes accessed | tf_op | source)
XLA Modules:
  0.0 42.4 jit_solution(6019095203612872918)
XLA Ops:
  0.6 39.4 %shard_map.119 = (f32[64,256]{1,0:T(8,128)}, bf16[2,1024,128]{2,1,0:T(8,128)(2,1)}) custom-call(bf16[1,1,64,256]{3,2,1,0:T(8,128)(2,1)} %feats_in.1, bf16[27,64,64]{2,1,0:T(8,128)(2,1)} %w1_in.1, f32[1,64]{1,0:T(1,128)} %bitcast.6, bf16[27,64,64]{2,1,0:T(8,128)(2,1)} %w2_in.1, f32[1,64]{1,0:T(1,128)} %bitcast.7, bf16[1,1,64,256]{3,2,1,0:T(8,128)(2,1)} %cot_in.1, ...), custom_call_target="tpu_custom_call" | custom-call | tf_op jit(solution)/shard_map/pallas_call | solution.py:531
  40.0 2.4 %shard_map.120 = (f32[1,1,64,256]{3,2,1,0:T(8,128)}, f32[27,64,64]{2,1,0:T(8,128)}, f32[1,64]{1,0:T(1,128)}, f32[27,64,64]{2,1,0:T(8,128)}, f32[1,64]{1,0:T(1,128)}) custom-call(f32[64,256]{1,0:T(8,128)} %get-tuple-element.12.gf_in, bf16[2,1024,128]{2,1,0:T(8,128)(2,1)} %get-tuple-element.13.full_in), custom_call_target="tpu_custom_call" | custom-call | tf_op jit(solution)/shard_map/pallas_call | solution.py:588
